TPU v7x, 32 devices: a whole 2x2x4 slice. The times are simulated.
32 devices in a mesh: dp: 16 (over z, y, x), mp: 2 (over core).
Axes of the slice: x: 2, y: 2, z: 4, core: 2. Of those that a mesh axis runs over, the one named last changes fastest.
Arguments:
- inputs: bfloat16 [21888, 512], P('dp'), may hold values from -6 to 6
- region_counts: int32 [96], P('dp'), may hold values from 10 to 100, as said below
- w_query: bfloat16 [512, 512], P(None, 'mp'), may hold values from -0.25 to 0.25
- b_query: float32 [512], P('mp'), may hold values from -3 to 3
- w_key: bfloat16 [512, 512], P(None, 'mp'), may hold values from -0.25 to 0.25
- w_value: bfloat16 [512, 512], P(None, 'mp'), may hold values from -0.25 to 0.25
- b_value: float32 [512], P('mp'), may hold values from -3 to 3
- w_out: bfloat16 [512, 512], P('mp'), may hold values from -3 to 3
- b_out: float32 [512], replicated, may hold values from -3 to 3
- gain_one: float32 [512], replicated, may hold values from 0.5 to 1.5
- shift_one: float32 [512], replicated, may hold values from -3 to 3
- w_up: bfloat16 [512, 2048], P(None, 'mp'), may hold values from -0.25 to 0.25
- b_up: float32 [2048], P('mp'), may hold values from -3 to 3
- w_down: bfloat16 [2048, 512], P('mp'), may hold values from -0.125 to 0.125
- b_down: float32 [512], replicated, may hold values from -3 to 3
- gain_two: float32 [512], replicated, may hold values from 0.5 to 1.5
- shift_two: float32 [512], replicated, may hold values from -3 to 3
- cotangent: float32 [21888, 512], P('dp'), may hold values from -6 to 6
Outputs:
- output: bfloat16 [21888, 512], P(('dp', 'mp'))
- input_grad: float32 [21888, 512], P(('dp', 'mp'))
- grad_w_query: float32 [512, 512], P('dp', 'mp')
- grad_b_query: float32 [512], P('mp')
- grad_w_key: float32 [512, 512], P('dp', 'mp')
- grad_w_value: float32 [512, 512], P('dp', 'mp')
- grad_b_value: float32 [512], P('mp')
- grad_w_out: float32 [512, 512], P('mp', 'dp')
- grad_b_out: float32 [512], replicated
- grad_gain_one: float32 [512], replicated
- grad_shift_one: float32 [512], replicated
- grad_w_up: float32 [512, 2048], P('dp', 'mp')
- grad_b_up: float32 [2048], P('mp')
- grad_w_down: float32 [2048, 512], P('mp', 'dp')
- grad_b_down: float32 [512], replicated
- grad_gain_two: float32 [512], replicated
- grad_shift_two: float32 [512], replicated
Inputs may be any that keep to these rules, and one draw needn't show every extreme that they name: `region_counts`: valid region slots of each item; some item has all 100 slots valid and some item has the fewest.
All inputs are finite; a program needn't handle non-finite values.
Results may differ from a plain program's by a relative error of at most 0.02.
Values may be sent and summed in bfloat16 or wider, within the bound.
A program may use at most 128 MiB of HBM per device.

v0:
```python
import jax
import jax.numpy as jnp
from jax import lax
from jax.sharding import PartitionSpec as P

HEAD_DIM = 64
TEXT = 128


def layer_stats(pre_rows):
    row_mean = jnp.mean(pre_rows, axis=-1, keepdims=True)
    centred = pre_rows - row_mean
    inverse = lax.rsqrt(jnp.mean(centred * centred, axis=-1, keepdims=True) + 1e-12)
    return (centred * inverse, inverse)


def norm_back(grad_rows, normed, inverse, gain_vec):
    scaled = grad_rows * gain_vec
    return inverse * (
        scaled
        - jnp.mean(scaled, axis=-1, keepdims=True)
        - normed * jnp.mean(scaled * normed, axis=-1, keepdims=True)
    )


def gelu_slope(upper_part):
    return (
        0.5 * (1.0 + lax.erf(upper_part * 0.7071067811865476))
        + upper_part * jnp.exp(-0.5 * upper_part * upper_part) * 0.3989422804014327
    )


def contract_rows(first_op, second_op):
    return lax.dot_general(
        first_op, second_op, (((0,), (0,)), ((), ())), preferred_element_type=jnp.float32
    )


def times_transposed(first_op, second_op):
    return lax.dot_general(
        first_op, second_op, (((1,), (1,)), ((), ())), preferred_element_type=jnp.float32
    )


def per_device(
    inputs,
    region_counts,
    w_query,
    b_query,
    w_key,
    w_value,
    b_value,
    w_out,
    b_out,
    gain_one,
    shift_one,
    w_up,
    b_up,
    w_down,
    b_down,
    gain_two,
    shift_two,
    cotangent,
):
    total_rows = inputs.shape[0]
    item_count = region_counts.shape[0]
    length = total_rows // item_count
    heads_here = w_query.shape[1] // HEAD_DIM
    score_scale = HEAD_DIM ** (-0.5)
    share_rows = total_rows // lax.axis_size("mp")
    row_start = lax.axis_index("mp") * share_rows

    def own_rows(full_rows):
        return lax.dynamic_slice_in_dim(full_rows, row_start, share_rows, 0)

    def split_heads(flat_rows):
        return flat_rows.reshape(item_count, length, heads_here, HEAD_DIM)

    position = jnp.arange(length)
    visible = (position[None, :] < TEXT) | (position[None, :] - TEXT < region_counts[:, None])
    key_mask = visible[:, None, None, :]
    queries = (jnp.dot(inputs, w_query, preferred_element_type=jnp.float32) + b_query).astype(
        jnp.bfloat16
    )
    key_rows = jnp.dot(inputs, w_key, preferred_element_type=jnp.float32).astype(jnp.bfloat16)
    value_rows = (jnp.dot(inputs, w_value, preferred_element_type=jnp.float32) + b_value).astype(
        jnp.bfloat16
    )
    query_heads = split_heads(queries)
    key_heads = split_heads(key_rows)
    value_heads = split_heads(value_rows)

    def masked_scores():
        raw_scores = (
            jnp.einsum(
                "ishd,ithd->ihst", query_heads, key_heads, preferred_element_type=jnp.float32
            )
            * score_scale
        )
        return jnp.where(key_mask, raw_scores, -1000000000.0)

    scores = masked_scores()
    row_top = jnp.max(scores, axis=-1, keepdims=True)
    exponent = jnp.exp(scores - row_top)
    row_total = jnp.sum(exponent, axis=-1, keepdims=True)
    probs = exponent / row_total
    log_total = row_top + jnp.log(row_total)
    context = jnp.einsum(
        "ihst,ithd->ishd",
        probs.astype(jnp.bfloat16),
        value_heads,
        preferred_element_type=jnp.float32,
    )
    context = context.reshape(total_rows, heads_here * HEAD_DIM).astype(jnp.bfloat16)
    partial_attn = jnp.dot(context, w_out, preferred_element_type=jnp.float32)
    attended = lax.psum(partial_attn, "mp")
    normed_one, inverse_one = layer_stats(attended + b_out + inputs.astype(jnp.float32))
    hidden_one = normed_one * gain_one + shift_one
    hidden_low = hidden_one.astype(jnp.bfloat16)
    upper_part = jnp.dot(hidden_low, w_up, preferred_element_type=jnp.float32) + b_up
    active = jax.nn.gelu(upper_part, approximate=False).astype(jnp.bfloat16)
    partial_ffn = jnp.dot(active, w_down, preferred_element_type=jnp.float32)
    lowered = lax.psum(partial_ffn, "mp")
    normed_two, inverse_two = layer_stats(lowered + b_down + hidden_one)
    output = own_rows(normed_two * gain_two + shift_two).astype(jnp.bfloat16)
    grad_pre_two = norm_back(cotangent, normed_two, inverse_two, gain_two)
    down_low = grad_pre_two.astype(jnp.bfloat16)
    grad_output = own_rows(cotangent)
    normed_two_own = own_rows(normed_two)
    grad_two_own = own_rows(grad_pre_two)
    grad_gain_two = jnp.sum(grad_output * normed_two_own, axis=0)
    grad_shift_two = jnp.sum(grad_output, axis=0)
    grad_b_down = jnp.sum(grad_two_own, axis=0)
    grad_w_down = contract_rows(active, down_low)
    active_grad = times_transposed(down_low, w_down)
    upper_grad = (active_grad * gelu_slope(upper_part)).astype(jnp.bfloat16)
    grad_b_up = jnp.sum(upper_grad.astype(jnp.float32), axis=0)
    grad_w_up = contract_rows(hidden_low, upper_grad)
    partial_hidden = times_transposed(upper_grad, w_up)
    hidden_grad = lax.psum(partial_hidden, "mp") + grad_pre_two
    grad_pre_one = norm_back(hidden_grad, normed_one, inverse_one, gain_one)
    out_low = grad_pre_one.astype(jnp.bfloat16)
    hidden_grad_own = own_rows(hidden_grad)
    normed_one_own = own_rows(normed_one)
    grad_one_own = own_rows(grad_pre_one)
    grad_gain_one = jnp.sum(hidden_grad_own * normed_one_own, axis=0)
    grad_shift_one = jnp.sum(hidden_grad_own, axis=0)
    grad_b_out = jnp.sum(grad_one_own, axis=0)
    grad_w_out = contract_rows(context, out_low)
    context_grad = split_heads(times_transposed(out_low, w_out).astype(jnp.bfloat16))
    probs_again = jnp.exp(masked_scores() - log_total)
    prob_grad = jnp.einsum(
        "ishd,ithd->ihst", context_grad, value_heads, preferred_element_type=jnp.float32
    )
    row_inner = jnp.sum(probs_again * prob_grad, axis=-1, keepdims=True)
    score_grad = (probs_again * (prob_grad - row_inner)).astype(jnp.bfloat16)
    query_grad = (
        (
            jnp.einsum("ihst,ithd->ishd", score_grad, key_heads, preferred_element_type=jnp.float32)
            * score_scale
        )
        .astype(jnp.bfloat16)
        .reshape(total_rows, heads_here * HEAD_DIM)
    )
    key_grad = (
        (
            jnp.einsum(
                "ihst,ishd->ithd", score_grad, query_heads, preferred_element_type=jnp.float32
            )
            * score_scale
        )
        .astype(jnp.bfloat16)
        .reshape(total_rows, heads_here * HEAD_DIM)
    )
    value_grad = jnp.einsum(
        "ihst,ishd->ithd",
        probs_again.astype(jnp.bfloat16),
        context_grad,
        preferred_element_type=jnp.float32,
    ).astype(jnp.bfloat16)
    value_grad = value_grad.reshape(total_rows, heads_here * HEAD_DIM)
    grad_b_query = jnp.sum(query_grad.astype(jnp.float32), axis=0)
    grad_b_value = jnp.sum(value_grad.astype(jnp.float32), axis=0)
    grad_w_query = contract_rows(inputs, query_grad)
    grad_w_key = contract_rows(inputs, key_grad)
    grad_w_value = contract_rows(inputs, value_grad)
    partial_input = (
        times_transposed(query_grad, w_query)
        + times_transposed(key_grad, w_key)
        + times_transposed(value_grad, w_value)
    )
    input_grad = own_rows(
        lax.psum(partial_input.astype(jnp.bfloat16), "mp").astype(jnp.float32) + grad_pre_one
    )
    bias_sums = lax.psum((grad_b_query, grad_b_value, grad_b_up), "dp")
    norm_sums = lax.psum(
        (grad_b_out, grad_gain_one, grad_shift_one, grad_b_down, grad_gain_two, grad_shift_two),
        ("dp", "mp"),
    )
    weight_sums = (
        lax.psum_scatter(
            grad_w_query.astype(jnp.bfloat16), "dp", scatter_dimension=0, tiled=True
        ).astype(jnp.float32),
        lax.psum_scatter(
            grad_w_key.astype(jnp.bfloat16), "dp", scatter_dimension=0, tiled=True
        ).astype(jnp.float32),
        lax.psum_scatter(
            grad_w_value.astype(jnp.bfloat16), "dp", scatter_dimension=0, tiled=True
        ).astype(jnp.float32),
        lax.psum_scatter(
            grad_w_out.astype(jnp.bfloat16), "dp", scatter_dimension=1, tiled=True
        ).astype(jnp.float32),
        lax.psum_scatter(
            grad_w_up.astype(jnp.bfloat16), "dp", scatter_dimension=0, tiled=True
        ).astype(jnp.float32),
        lax.psum_scatter(
            grad_w_down.astype(jnp.bfloat16), "dp", scatter_dimension=1, tiled=True
        ).astype(jnp.float32),
    )
    return (
        output,
        input_grad,
        weight_sums[0],
        bias_sums[0],
        weight_sums[1],
        weight_sums[2],
        bias_sums[1],
        weight_sums[3],
        norm_sums[0],
        norm_sums[1],
        norm_sums[2],
        weight_sums[4],
        bias_sums[2],
        weight_sums[5],
        norm_sums[3],
        norm_sums[4],
        norm_sums[5],
    )


def solution(mesh):
    placed = (
        P("dp", None),
        P("dp"),
        P(None, "mp"),
        P("mp"),
        P(None, "mp"),
        P(None, "mp"),
        P("mp"),
        P("mp", None),
        P(),
        P(),
        P(),
        P(None, "mp"),
        P("mp"),
        P("mp", None),
        P(),
        P(),
        P(),
        P("dp", None),
    )
    return jax.shard_map(
        per_device,
        mesh=mesh,
        in_specs=placed,
        out_specs=(
            P(("dp", "mp"), None),
            P(("dp", "mp"), None),
            P("dp", "mp"),
            P("mp"),
            P("dp", "mp"),
            P("dp", "mp"),
            P("mp"),
            P("mp", "dp"),
            P(),
            P(),
            P(),
            P("dp", "mp"),
            P("mp"),
            P("mp", "dp"),
            P(),
            P(),
            P(),
        ),
        check_vma=False,
    )
```

profile of v0, /device:TPU:0, one launch (start us, length us, event | category | flops | bytes accessed | tf_op | source)
XLA Modules:
  0.0 679.5 jit_solution(1611943066500404588)
XLA Ops:
  11.0 3.3 copy.76
  16.5 3.3 copy.78
  34.5 3.3 fusion.49
  38.1 25.2 %all-reduce.7.cloned.1.call-done = f32[1368,512]{1,0:T(8,128)} async-done(((f32[1368,512]{1,0:T(8,128)}), f32[1368,512]{1,0:T(8,128)}) %all-reduce.7.cloned.1.call-update) | async-done | bytes 2801680 | tf_op jit(solution)/shard_map/psum | solution.py:116
  67.4 14.9 %fusion.2 = (bf16[1368,1024]{1,0:T(8,128)(2,1)S(1)}, f32[1368,1024]{1,0:T(8,128)}) fusion(f32[1024]{0:T(1024)S(1)} %copy-done.38, bf16[512,1024]{1,0:T(8,128)(2,1)S(1)} %copy-done, f32[1368,512]{1,0:T(8,128)S(1)} %subtract_multiply_fusion.3, f32[512]{0:T(512)S(1)} %copy-done.29, f32[512]{0:T(512)S(1)} %copy-done.26), kind=kOutput, calls=%fused_computation.10 | convolution fusion | flops 1529008128 | bytes 12263424 | tf_op jit(solution)/shard_map/dot_general | solution.py:120
  83.9 3.2 fusion.50
  87.2 23.8 %all-reduce.9.cloned.1.call-done = f32[1368,512]{1,0:T(8,128)} async-done(((f32[1368,512]{1,0:T(8,128)}), f32[1368,512]{1,0:T(8,128)}) %all-reduce.9.cloned.1.call-update) | async-done | bytes 2801680 | tf_op jit(solution)/shard_map/psum | solution.py:123
  111.1 3.2 fusion.47
  119.4 4.6 convert_reduce_fusion
  125.6 3.3 fusion.51
  128.9 5.5 convolution_convert_fusion.2
  134.8 6.4 convolution_convert_fusion.3
  141.2 11.5 %all-reduce.11.cloned.1.call-done = f32[1368,512]{1,0:T(8,128)} async-done(((f32[1368,512]{1,0:T(8,128)}), f32[1368,512]{1,0:T(8,128)}) %all-reduce.11.cloned.1.call-update) | async-done | bytes 2801680 | tf_op jit(solution)/shard_map/psum | solution.py:140
  152.7 4.3 multiply_reduce_fusion.5
  164.9 3.8 convert_reduce_fusion.1
  177.0 6.8 multiply_reduce_fusion
  183.9 5.6 multiply_convert_fusion
  193.5 2.8 reshape.169
  204.8 2.8 reshape.168
  211.9 3.2 convolution_convert_fusion.4
  215.1 3.2 fusion.52
  224.2 3.1 dynamic-slice_reduce_fusion.2
  227.3 6.6 reduce-scatter.17.cloned.1.call-done
  235.4 74.8 %reduce-scatter.15.cloned.1.call-done = bf16[32,1024]{1,0:T(8,128)(2,1)} async-done(((bf16[512,1024]{1,0:T(8,128)(2,1)}), bf16[32,1024]{1,0:T(8,128)(2,1)}) %reduce-scatter.15.cloned.1.call-update) | async-done | bytes 65552 | tf_op jit(solution)/shard_map/reduce_scatter | solution.py:213
  311.9 38.3 %all-reduce.1 = (f32[256]{0:T(256)}, f32[256]{0:T(256)}, f32[1024]{0:T(1024)}) all-reduce(f32[256]{0:T(256)S(1)} %reduce_sum.186, f32[256]{0:T(256)S(1)} %reduce_sum.188, f32[1024]{0:T(1024)S(1)} %copy-done.32), channel_id=1, replica_groups=mesh['dp'=16,'mp'=2] {'dp'}, use_global_device_ids=true, to_apply=%region_17.18 | all-reduce | flops 1536 | bytes 12288 | tf_op jit(solution)/shard_map/psum | solution.py:195
  352.3 32.6 %reduce-scatter.23.cloned.1.call-done = bf16[32,256]{1,0:T(8,128)(2,1)} async-done(((bf16[512,256]{1,0:T(8,128)(2,1)}), bf16[32,256]{1,0:T(8,128)(2,1)}) %reduce-scatter.23.cloned.1.call-update) | async-done | bytes 16400
  386.5 73.3 %reduce-scatter.21.cloned.1.call-done = bf16[32,256]{1,0:T(8,128)(2,1)} async-done(((bf16[512,256]{1,0:T(8,128)(2,1)}), bf16[32,256]{1,0:T(8,128)(2,1)}) %reduce-scatter.21.cloned.1.call-update) | async-done | bytes 16400
  461.3 73.2 %reduce-scatter.19.cloned.1.call-done = bf16[32,256]{1,0:T(8,128)(2,1)} async-done(((bf16[512,256]{1,0:T(8,128)(2,1)}), bf16[32,256]{1,0:T(8,128)(2,1)}) %reduce-scatter.19.cloned.1.call-update) | async-done | bytes 16400
  536.0 73.1 %reduce-scatter.13.cloned.1.call-done = bf16[256,32]{0,1:T(8,128)(2,1)} async-done(((bf16[256,512]{0,1:T(8,128)(2,1)}), bf16[256,32]{0,1:T(8,128)(2,1)}) %reduce-scatter.13.cloned.1.call-update) | async-done | bytes 16400 | tf_op jit(solution)/shard_map/reduce_scatter | solution.py:210
  610.4 18.1 %all-reduce.13.cloned.1.call-done = bf16[1368,512]{1,0:T(8,128)(2,1)} async-done(((bf16[1368,512]{1,0:T(8,128)(2,1)}), bf16[1368,512]{1,0:T(8,128)(2,1)}) %all-reduce.13.cloned.1.call-update) | async-done | bytes 1400848 | tf_op jit(solution)/shard_map/psum | solution.py:193
  628.6 2.9 dynamic-slice_reduce_fusion.1
  631.5 40.7 %all-reduce = (f32[512]{0:T(512)}, f32[512]{0:T(512)}, f32[512]{0:T(512)}, f32[512]{0:T(512)}, f32[512]{0:T(512)}, /*index=5*/f32[512]{0:T(512)}) all-reduce(f32[512]{0:T(512)S(1)} %get-tuple-element.90, f32[512]{0:T(512)S(1)} %get-tuple-element.75, f32[512]{0:T(512)S(1)} %get-tuple-element.74, ...), channel_id=1, replica_groups=mesh['dp'=16,'mp'=2] {'dp','mp'}, use_global_device_ids=true, to_apply=%region_24.25 | all-reduce | flops 3072 | bytes 24576 | tf_op jit(solution)/shard_map/psum | solution.py:196
  (167 shorter events, 83.7 us)
Async XLA Ops:
  7.2 60.1 %copy-start = (bf16[512,1024]{1,0:T(8,128)(2,1)S(1)}, bf16[512,1024]{1,0:T(8,128)(2,1)}, u32[]{:S(2)}) copy-start(bf16[512,1024]{1,0:T(8,128)(2,1)} %param.29) | copy-start | bytes 3145732
  7.2 56.1 %all-reduce.7.cloned.1.call-start = ((), (), s32[]{:S(2)}) async-start(), calls=%async_computation.6 | async-start | bytes 5603328 | tf_op jit(solution)/shard_map/psum | solution.py:116
  9.3 5.0 copy-start.7
  9.3 5.0 copy-start.24
  9.3 5.0 copy-start.39
  14.9 5.0 copy-start.22
  19.9 4.7 copy-start.35
  34.5 3.4 copy-start.15
  34.5 28.8 %copy-start.30 = (f32[512]{0:T(512)S(1)}, f32[512]{0:T(512)}, u32[]{:S(2)}) copy-start(f32[512]{0:T(512)} %param.26) | copy-start | bytes 6148
  37.9 73.2 %all-reduce.9.cloned.1.call-start = ((), (), s32[]{:S(2)}) async-start(), calls=%async_computation.7 | async-start | bytes 5603328 | tf_op jit(solution)/shard_map/psum | solution.py:123
  67.4 14.9 %copy-start.2 = (f32[1368,512]{1,0:T(8,128)}, f32[1368,512]{1,0:T(8,128)S(1)}, u32[]{:S(2)}) copy-start(f32[1368,512]{1,0:T(8,128)S(1)} %subtract_multiply_fusion.3) | copy-start | bytes 8404996
  67.4 16.5 %copy-start.36 = (bf16[1024,512]{1,0:T(8,128)(2,1)S(1)}, bf16[1024,512]{1,0:T(8,128)(2,1)}, u32[]{:S(2)}) copy-start(bf16[1024,512]{1,0:T(8,128)(2,1)} %param.31) | copy-start | bytes 3145732
  87.2 23.9 %copy-start.33 = (f32[512]{0:T(512)S(1)}, f32[512]{0:T(512)}, u32[]{:S(2)}) copy-start(f32[512]{0:T(512)} %param.32) | copy-start | bytes 6148
  87.2 65.5 %all-reduce.11.cloned.1.call-start = ((), (), s32[]{:S(2)}) async-start(), calls=%async_computation.8 | async-start | bytes 5603328 | tf_op jit(solution)/shard_map/psum | solution.py:140
  114.3 4.5 slice-start
  118.8 5.2 copy-start.8
  128.8 5.9 copy-start.28
  128.9 105.1 %reduce-scatter.17.cloned.1.call-start = ((), (), s32[]{:S(2)}) async-start(), calls=%async_computation.12 | async-start | bytes 1114112 | tf_op jit(solution)/shard_map/reduce_scatter | solution.py:216
  134.5 175.7 %reduce-scatter.15.cloned.1.call-start = ((), (), s32[]{:S(2)}) async-start(), calls=%async_computation.11 | async-start | bytes 1114112 | tf_op jit(solution)/shard_map/reduce_scatter | solution.py:213
  141.2 243.8 %reduce-scatter.23.cloned.1.call-start = ((), (), s32[]{:S(2)}) async-start(), calls=%async_computation.15 | async-start | bytes 278528
  152.7 4.3 copy-start.3
  183.8 276.0 %reduce-scatter.21.cloned.1.call-start = ((), (), s32[]{:S(2)}) async-start(), calls=%async_computation.14 | async-start | bytes 278528
  183.9 7.2 %copy-start.14 = (bf16[6,228,4,64]{1,3,2,0:T(8,128)(2,1)S(1)}, bf16[6,228,4,64]{1,3,2,0:T(8,128)(2,1)}, u32[]{:S(2)}) copy-start(bf16[6,228,4,64]{1,3,2,0:T(8,128)(2,1)} %copy.76) | copy-start | bytes 2101252
  193.5 7.3 %copy-start.13 = (bf16[6,228,4,64]{1,3,2,0:T(8,128)(2,1)S(1)}, bf16[6,228,4,64]{1,3,2,0:T(8,128)(2,1)}, u32[]{:S(2)}) copy-start(bf16[6,228,4,64]{1,3,2,0:T(8,128)(2,1)} %copy-done.12) | copy-start | bytes 2101252
  200.4 334.0 %reduce-scatter.19.cloned.1.call-start = ((), (), s32[]{:S(2)}) async-start(), calls=%async_computation.13 | async-start | bytes 278528
  204.7 7.1 %copy-start.16 = (bf16[1368,256]{0,1:T(8,128)(2,1)S(1)}, bf16[1368,256]{0,1:T(8,128)(2,1)}, u32[]{:S(2)}) copy-start(bf16[1368,256]{0,1:T(8,128)(2,1)} %copy-done.15) | copy-start | bytes 2101252
  209.9 5.2 copy-start.20
  211.8 397.3 %reduce-scatter.13.cloned.1.call-start = ((), (), s32[]{:S(2)}) async-start(), calls=%async_computation.10 | async-start | bytes 278528 | tf_op jit(solution)/shard_map/reduce_scatter | solution.py:210
  215.1 3.3 copy-start.19
  218.3 410.2 %all-reduce.13.cloned.1.call-start = ((), (), s32[]{:S(2)}) async-start(), calls=%async_computation.9 | async-start | bytes 2801664 | tf_op jit(solution)/shard_map/psum | solution.py:193
  220.9 3.3 copy-start.34
  222.6 89.3 %copy-start.32 = (f32[1024]{0:T(1024)S(1)}, f32[1024]{0:T(1024)}, u32[]{:S(2)}) copy-start(f32[1024]{0:T(1024)} %get-tuple-element.102) | copy-start | bytes 12292
  (21 other events, 39.5 us)
Sparse Core Ops, SparseCore 0:
  38.0 25.2 all-reduce.6
  87.3 23.6 all-reduce.8
  129.0 23.6 all-reduce.10
  154.9 78.9 reduce-scatter.16
  236.0 74.1 reduce-scatter.14
  312.4 72.5 reduce-scatter.22
  387.2 72.5 reduce-scatter.20
  462.1 72.3 reduce-scatter.18
  536.7 72.3 reduce-scatter.12
  612.0 16.4 all-reduce.12
where the time goes:
time: 687 us; the launch traced here: 679 us
  waiting for transfers between devices  412 us (60%)
  matrix products  80.6 us (12%)
  blocking collectives  79 us (11%)
  local copies, waits for them, and re-layouts  55 us (8%)
  other arithmetic  36.4 us (5%)
  between operations  15.2 us (2%)
    unnamed x13, waiting for transfers between devices  179 us
    reduce_scatter x1, waiting for transfers between devices, per_device(): lax.psum_scatter(grad_w_up.astype(jnp.bfloat16), 'dp', scatter_dimension=...  74.8 us
    reduce_scatter x1, waiting for transfers between devices, per_device(): lax.psum_scatter(grad_w_out.astype(jnp.bfloat16), 'dp', scatter_dimension...  73.1 us
    psum x1, blocking collectives, per_device(): lax.psum((grad_b_out, grad_gain_one, grad_shift_one, grad_b_down, grad_ga...  40.7 us
    psum x1, blocking collectives, per_device(): bias_sums = lax.psum((grad_b_query, grad_b_value, grad_b_up), 'dp')  38.3 us
    psum x1, waiting for transfers between devices, per_device(): attended = lax.psum(partial_attn, 'mp')  25.2 us
    psum x1, waiting for transfers between devices, per_device(): lowered = lax.psum(partial_ffn, 'mp')  23.8 us
    dot_general x6, matrix products, contract_rows(): lax.dot_general(first_op, second_op, (((0,), (0,)), ((), ())), preferred_...  22.3 us
  transfers between devices with their start and end apart: 10, of which 10 were waited for; matrix products, arithmetic and copies ran while one was open for 14% of the time, Pallas kernels for 0%

commit v1 on v0

--- a/solution.py
+++ b/solution.py
@@ -1,6 +1,11 @@
+import functools
+import types
+
 import jax
 import jax.numpy as jnp
 from jax import lax
+from jax.experimental import pallas as pl
+from jax.experimental.pallas import tpu as pltpu
 from jax.sharding import PartitionSpec as P
 
 HEAD_DIM = 64
@@ -238,6 +243,642 @@
     )
 
 
+ITEM_PAD = 16
+MESH = pl.DeviceIdType.MESH
+BF = jnp.bfloat16
+F32 = jnp.float32
+BLOCK = 256
+UNITS = 12
+X_FIRST, Y_FIRST, LOW_FIRST, HIGH_FIRST = 0, 1, 2, 3
+ORDER = (0, 1, 2, 3, 0, 1, 2, 3, 0, 1, 2, 3)
+
+
+def dot_nn(a, b):
+    return lax.dot_general(a, b, (((1,), (0,)), ((), ())), preferred_element_type=F32)
+
+
+def dot_nt(a, b):
+    return lax.dot_general(a, b, (((1,), (1,)), ((), ())), preferred_element_type=F32)
+
+
+def layer_kernel(dims, names, *refs):
+    r = types.SimpleNamespace(**dict(zip(names, refs, strict=True)))
+    items, length, rows_pad, lanes, nz, shard = dims
+    total = items * rows_pad
+    chunks = r.wu_h.shape[1] // BLOCK
+    width = r.x_h.shape[1]
+    dp, mp = lax.axis_index("dp"), lax.axis_index("mp")
+    z, y, x = dp // 4, (dp // 2) % 2, dp % 2
+
+    def at(z_, y_, x_):
+        return z_ * 4 + y_ * 2 + x_
+
+    core = (dp, 1 - mp)
+    x_side = (at(z, y, 1 - x), mp)
+    y_side = (at(z, 1 - y, x), mp)
+    z_side = [(at((z + step) % nz, y, x), mp) for step in range(1, nz)]
+    low_side = (at(z + 1 - 2 * (z % 2), y, x), mp)
+    high_side = (at(nz - 1 - z, y, x), mp)
+    plane_side = [(at(z, (y + step // 2) % 2, (x + step) % 2), mp) for step in range(1, 4)]
+
+    local = []
+
+    def bring(src, dst):
+        copy = pltpu.make_async_copy(src, dst, r.in_sem.at[len(local)])
+        copy.start()
+        local.append(copy)
+        return copy
+
+    c_x = bring(r.x_h, r.x_raw)
+    c_w = [bring(src, r.wqkv.at[0, k]) for k, src in enumerate((r.wq_h, r.wk_h, r.wv_h))]
+    c_p = [bring(r.b_query_h, r.bias_q.at[0]), bring(r.b_value_h, r.bias_v.at[0]), bring(r.b_up_h, r.bias_u.at[0])]
+    vectors = (
+        (r.b_out_h, r.b_out), (r.gain_one_h, r.gain_one), (r.shift_one_h, r.shift_one),
+        (r.b_down_h, r.b_down), (r.gain_two_h, r.gain_two), (r.shift_two_h, r.shift_two))
+    c_vec = [bring(src, dst) for src, dst in vectors]
+    c_wo = bring(r.wo_h, r.wo.at[0])
+    c_wu = [bring(r.wu_h.at[:, pl.ds(c * BLOCK, BLOCK)], r.wu.at[c]) for c in range(chunks)]
+    c_wd = bring(r.wd_h, r.wd.at[pl.ds(0, chunks)])
+    full_rows = r.cot_h.shape[0]
+    c_cot = bring(r.cot_h, r.cot_raw.at[pl.ds(0, full_rows)])
+
+    barrier = pltpu.get_barrier_semaphore()
+    near = [core] + plane_side + z_side
+    for device in near:
+        pl.semaphore_signal(barrier, inc=1, device_id=device, device_id_type=MESH)
+    pl.semaphore_wait(barrier, len(near))
+
+    remote = []
+
+    def send_weight(src, dst):
+        k = len(remote)
+        copy = pltpu.make_async_remote_copy(
+            src_ref=src, dst_ref=dst, send_sem=r.w_send.at[k], recv_sem=r.w_recv.at[k],
+            device_id=core, device_id_type=MESH)
+        copy.start()
+        remote.append(copy)
+        return copy
+
+    s_w = [send_weight(src, r.wqkv.at[1, k]) for k, src in enumerate((r.wq_h, r.wk_h, r.wv_h))]
+    s_w += [send_weight(src, dst.at[1]) for src, dst in (
+        (r.b_query_h, r.bias_q), (r.b_value_h, r.bias_v), (r.b_up_h, r.bias_u))]
+    s_wo = send_weight(r.wo_h, r.wo.at[1])
+    s_wu = [send_weight(r.wu_h.at[:, pl.ds(c * BLOCK, BLOCK)], r.wu.at[chunks + c]) for c in range(chunks)]
+    s_wd = send_weight(r.wd_h, r.wd.at[pl.ds(chunks, chunks)])
+
+    pad_rows = lanes - rows_pad
+
+    def transposed(block):
+        full = jnp.concatenate([block, jnp.zeros((pad_rows, block.shape[1]), F32)], axis=0)
+        return full.T.astype(BF)
+
+    def rows_of(i):
+        return pl.ds(pl.multiple_of(i * rows_pad, 16), rows_pad)
+
+    def lanes_of(i):
+        return pl.ds(pl.multiple_of(i * lanes, lanes), lanes)
+
+    def clear(n, carry):
+        r.probs[n, pl.ds(rows_pad, pad_rows), :] = jnp.zeros((pad_rows, lanes), BF)
+        return carry
+
+    lax.fori_loop(0, r.probs.shape[0], clear, 0)
+    zero_block = jnp.zeros((pad_rows, BLOCK), BF)
+    for i in range(items):
+        r.upg[i, pl.ds(rows_pad, pad_rows), :] = zero_block
+        r.olow[i, pl.ds(rows_pad, pad_rows), :] = jnp.zeros((pad_rows, r.olow.shape[2]), BF)
+        for j in range(2 * chunks):
+            r.active[j, i, pl.ds(rows_pad, pad_rows), :] = zero_block
+    for k in range(2):
+        r.dscore[k, pl.ds(rows_pad, pad_rows), :] = jnp.zeros((pad_rows, lanes), BF)
+    one_row = jnp.where(lax.broadcasted_iota(jnp.int32, (16, items * lanes), 0) == 0, 1.0, 0.0).astype(BF)
+    r.xT[pl.ds(width, 16), :] = one_row
+    r.hT[pl.ds(width, 16), :] = one_row
+
+    cot_rows = r.cot_raw.shape[0]
+    r.cot_raw[pl.ds(full_rows, cot_rows - full_rows), :] = jnp.zeros((cot_rows - full_rows, width), F32)
+
+    c_x.wait()
+    down_ = lax.broadcasted_iota(jnp.int32, (rows_pad, 256), 0)
+    across = lax.broadcasted_iota(jnp.int32, (rows_pad, 256), 1)
+    for i in range(items):
+        block = None
+        for m in range(2):
+            start = (m * items + i) * length
+            window = start // 16 * 16
+            count = min(256, full_rows - window)
+            shift = jnp.where(mp == m, start - window, 2 * 256)
+            pick = jnp.where((across == down_ + shift) & (down_ < length), 1.0, 0.0).astype(BF)
+            term = dot_nn(pick[:, :count], r.x_raw[pl.ds(window, count), :])
+            block = term if block is None else block + term
+        r.x_v[rows_of(i), :] = block.astype(BF)
+        r.xT[pl.ds(0, width), lanes_of(i)] = transposed(block)
+
+    def project(slot):
+        def one(k, carry):
+            shift = jnp.where(k == 0, r.bias_q[slot], jnp.where(k == 2, r.bias_v[slot], 0.0))
+            acc = dot_nn(r.x_v[...], r.wqkv[slot, k]) + shift
+            for i in range(items):
+                block = acc[i * rows_pad:(i + 1) * rows_pad]
+                r.nat[slot * items + i, k] = block.astype(BF)
+                low = block.astype(BF).astype(F32)
+                r.tra[slot * items + i, k] = transposed(low * jnp.where(k == 2, 1.0, 0.125))
+            return carry
+
+        lax.fori_loop(0, 3, one, 0)
+
+    for c in c_w + c_p:
+        c.wait()
+    project(0)
+    for s in s_w:
+        s.wait_recv()
+    project(1)
+
+    lane = lax.broadcasted_iota(jnp.int32, (1, 128), 1)
+    half = [jnp.where(lane < 64, 1.0, 0.0).astype(BF), jnp.where(lane >= 64, 1.0, 0.0).astype(BF)]
+
+    position = lax.broadcasted_iota(jnp.int32, (rows_pad, lanes), 0)
+
+    def attend(n, carry):
+        i = lax.rem(n, items)
+        mask = jnp.where(position < TEXT + r.counts[mp * items + i], 0.0, -1e9)
+        parts = []
+        for h in range(4):
+            pair = slice((h // 2) * 128, (h // 2) * 128 + 128)
+            keys = r.nat[n, 1, :, pair] * half[h % 2]
+            score = dot_nn(keys, r.tra[n, 0, pair, :]) + mask
+            top = jnp.max(score, axis=0, keepdims=True)
+            e = jnp.exp(score - top)
+            p = e * (1.0 / jnp.sum(e, axis=0, keepdims=True))
+            r.probs[n * 4 + h, pl.ds(0, rows_pad), :] = p.astype(BF)
+            parts.append(dot_nn(r.tra[n, 2, h * 64:(h + 1) * 64, :], r.probs[n * 4 + h]))
+        context = jnp.concatenate(parts, axis=0)
+        slot = n // items
+        r.ctxT[slot, :, lanes_of(i)] = context.astype(BF)
+        r.ctx[slot, rows_of(i), :] = context.T[:rows_pad].astype(BF)
+        return carry
+
+    lax.fori_loop(0, 2 * items, attend, 0)
+
+    c_wo.wait()
+    s_wo.wait_recv()
+    for c in c_vec:
+        c.wait()
+
+    def first_norm(i, carry):
+        att = dot_nn(r.ctx[0, rows_of(i), :], r.wo[0]) + dot_nn(r.ctx[1, rows_of(i), :], r.wo[1])
+        pre = att + r.b_out[...] + r.x_v[rows_of(i), :].astype(F32)
+        centred = pre - jnp.mean(pre, axis=1, keepdims=True)
+        inverse = lax.rsqrt(jnp.mean(centred * centred, axis=1, keepdims=True) + 1e-12)
+        normed = centred * inverse
+        r.n1[rows_of(i), :] = normed
+        r.inv1[rows_of(i), :] = jnp.broadcast_to(inverse, (rows_pad, 128))
+        hidden = normed * r.gain_one[...] + r.shift_one[...]
+        r.hlow[rows_of(i), :] = hidden.astype(BF)
+        r.hT[pl.ds(0, width), lanes_of(i)] = transposed(hidden)
+        return carry
+
+    lax.fori_loop(0, items, first_norm, 0)
+
+    for c in c_wu + [c_wd]:
+        c.wait()
+    for s in s_wu + [s_wd]:
+        s.wait_recv()
+    r.acc[...] = jnp.zeros(r.acc.shape, F32)
+
+    def feed(j, carry):
+        slot, c = j // chunks, lax.rem(j, chunks)
+        up_bias = r.bias_u[slot, :, pl.ds(pl.multiple_of(c * BLOCK, BLOCK), BLOCK)]
+        for i in range(items):
+            u = dot_nn(r.hlow[rows_of(i), :], r.wu[j]) + up_bias
+            phi = 0.5 + 0.5 * lax.erf(u * 0.7071067811865476)
+            r.slope[j, rows_of(i), :] = (phi + u * (jnp.exp(-0.5 * u * u) * 0.3989422804014327)).astype(BF)
+            act = (u * phi).astype(BF)
+            r.active[j, i, pl.ds(0, rows_pad), :] = act
+            r.acc[rows_of(i), :] += dot_nn(act, r.wd[j])
+        return carry
+
+    lax.fori_loop(0, 2 * chunks, feed, 0)
+
+    c_cot.wait()
+    sums = [None, None, None]
+
+    valid = lax.broadcasted_iota(jnp.int32, (rows_pad, 1), 0) < length
+
+    def second_norm(i, carry):
+        gain2, shift2, bdown = carry
+        hidden = r.n1[rows_of(i), :] * r.gain_one[...] + r.shift_one[...]
+        pre = r.acc[rows_of(i), :] + r.b_down[...] + hidden
+        centred = pre - jnp.mean(pre, axis=1, keepdims=True)
+        inverse = lax.rsqrt(jnp.mean(centred * centred, axis=1, keepdims=True) + 1e-12)
+        normed = centred * inverse
+        r.out_f[pl.ds(i * length, rows_pad), :] = normed * r.gain_two[...] + r.shift_two[...]
+        pieces = [r.cot_raw[pl.ds((m * items + i) * length, rows_pad), :] for m in range(2)]
+        cot = jnp.where(valid, jnp.where(mp == 0, pieces[0], pieces[1]), 0.0)
+        g = cot * r.gain_two[...]
+        grad = inverse * (
+            g - jnp.mean(g, axis=1, keepdims=True) - normed * jnp.mean(g * normed, axis=1, keepdims=True))
+        r.gp[rows_of(i), :] = grad
+        r.dlow[rows_of(i), :] = grad.astype(BF)
+        r.dT[:, lanes_of(i)] = transposed(grad)
+        return (gain2 + jnp.sum(cot * normed, axis=0, keepdims=True),
+                shift2 + jnp.sum(cot, axis=0, keepdims=True),
+                bdown + jnp.sum(grad, axis=0, keepdims=True))
+
+    zero_vec = jnp.zeros((1, width), F32)
+    carry = (zero_vec, zero_vec, zero_vec)
+    for i in range(items):
+        carry = second_norm(i, carry)
+    gain2, shift2, bdown = carry
+    r.out_v[...] = r.out_f[pl.ds(0, items * length), :].astype(BF)
+    out_copy = pltpu.make_async_copy(r.out_v, r.out_h, r.out_sem.at[0])
+    out_copy.start()
+
+    def to_core(u):
+        return pltpu.make_async_remote_copy(
+            src_ref=r.g_out.at[u], dst_ref=r.g_core.at[u], send_sem=r.core_send.at[u],
+            recv_sem=r.core_recv.at[u], device_id=core, device_id_type=MESH)
+
+    place_z = jnp.where(z == 0, 0, jnp.where(z == nz - 1, 1, z + 1))
+    route = (
+        (x, y, z, x_side, y_side), (y, x, z, y_side, x_side),
+        (place_z // 2, place_z % 2, y * 2 + x, low_side, high_side), (z // 2, z % 2, y * 2 + x, high_side, low_side))
+    shards = 4 * nz
+
+    def shard_order(order):
+        if order == X_FIRST:
+            return [at(c, b, a) for a in range(2) for b in range(2) for c in range(nz)]
+        if order == Y_FIRST:
+            return [at(c, a, b) for a in range(2) for b in range(2) for c in range(nz)]
+        ring = (0, nz - 1, 1, 2) if order == LOW_FIRST else (0, 1, 2, 3)
+        return [at(c, b, a) for c in ring for b in range(2) for a in range(2)]
+
+    def stage_a(u, order):
+        first, _, _, device, _ = route[order]
+        return pltpu.make_async_remote_copy(
+            src_ref=r.g.at[u, pl.ds((1 - first) * 8, 8)], dst_ref=r.g_a.at[u], send_sem=r.a_send.at[u],
+            recv_sem=r.a_recv.at[u], device_id=device, device_id_type=MESH)
+
+    def stage_b(u, order):
+        first, second, _, _, device = route[order]
+        return pltpu.make_async_remote_copy(
+            src_ref=r.g.at[u, pl.ds(first * 8 + (1 - second) * 4, 4)], dst_ref=r.g_b.at[u], send_sem=r.b_send.at[u],
+            recv_sem=r.b_recv.at[u], device_id=device, device_id_type=MESH)
+
+    def stage_c(u, order, step):
+        first, second, _, _, _ = route[order]
+        if order in (X_FIRST, Y_FIRST):
+            place, device = (z + step) % nz, z_side[step - 1]
+        else:
+            place, device = ((y + step // 2) % 2) * 2 + (x + step) % 2, plane_side[step - 1]
+        return pltpu.make_async_remote_copy(
+            src_ref=r.g.at[u, first * 8 + second * 4 + place], dst_ref=r.g_c.at[u, step - 1],
+            send_sem=r.c_send.at[u, step - 1], recv_sem=r.c_recv.at[u, step - 1],
+            device_id=device, device_id_type=MESH)
+
+    def start_core(u, value):
+        r.g_out[u] = value.astype(BF)
+        to_core(u).start()
+
+    def start_a(u, value, order):
+        to_core(u).wait_recv()
+        total_ = (value + r.g_core[u].astype(F32)).astype(BF)
+        for place, block in enumerate(shard_order(order)):
+            r.g[u, place] = total_[block * shard:(block + 1) * shard]
+        stage_a(u, order).start()
+
+    def start_b(u):
+        order = ORDER[u]
+        stage_a(u, order).wait()
+        kept = pl.ds(route[order][0] * 8, 8)
+        r.g[u, kept] = r.g[u, kept] + r.g_a[u]
+        stage_b(u, order).start()
+
+    def start_c(u):
+        order = ORDER[u]
+        stage_b(u, order).wait()
+        kept = pl.ds(route[order][0] * 8 + route[order][1] * 4, 4)
+        r.g[u, kept] = r.g[u, kept] + r.g_b[u]
+        for step in range(1, 4):
+            stage_c(u, order, step).start()
+
+    def finish(u):
+        order = ORDER[u]
+        first, second, third, _, _ = route[order]
+        acc = r.g[u, first * 8 + second * 4 + third].astype(F32)
+        for step in range(1, 4):
+            stage_c(u, order, step).wait()
+            acc += r.g_c[u, step - 1].astype(F32)
+        return acc
+
+    def vec_copy(k, stage, src, device):
+        return pltpu.make_async_remote_copy(
+            src_ref=src, dst_ref=r.v_in.at[k, stage], send_sem=r.v_send.at[k, stage],
+            recv_sem=r.v_recv.at[k, stage], device_id=device, device_id_type=MESH)
+
+    def vec_core(k):
+        return vec_copy(k, 0, r.v_out.at[k], core)
+
+    def vec_side(k, stage):
+        return vec_copy(k, stage, r.v_sum.at[k, stage - 1], (x_side, y_side)[stage - 1])
+
+    def vec_z(k, step):
+        return vec_copy(k, 2 + step, r.v_sum.at[k, 2], z_side[step - 1])
+
+    def vec_next(k, stage):
+        if stage == 0:
+            vec_core(k).wait()
+            r.v_sum[k, 0] = r.v_own[k] + r.v_in[k, 0]
+            vec_side(k, 1).start()
+        elif stage == 1:
+            vec_side(k, 1).wait()
+            r.v_sum[k, 1] = r.v_sum[k, 0] + r.v_in[k, 1]
+            vec_side(k, 2).start()
+        elif stage == 2:
+            vec_side(k, 2).wait()
+            r.v_sum[k, 2] = r.v_sum[k, 1] + r.v_in[k, 2]
+            for step in range(1, nz):
+                vec_z(k, step).start()
+        else:
+            for step in range(1, nz):
+                vec_z(k, step).wait()
+            terms = [r.v_sum[k, 2]] + [r.v_in[k, 2 + step] for step in range(1, nz)]
+            acc = jnp.zeros(terms[0].shape, F32)
+            for zz in range(nz):
+                came = lax.rem(z - zz + nz, nz)
+                term = terms[0]
+                for step in range(1, nz):
+                    term = jnp.where(came == step, terms[step], term)
+                acc = acc + term
+            if k == 0:
+                for j, ref in enumerate((r.bout_o, r.gain1_o, r.shift1_o, r.bdown_o, r.gain2_o, r.shift2_o)):
+                    for part in range(2):
+                        ref[:, part * BLOCK:(part + 1) * BLOCK] = acc[2 * j + part:2 * j + part + 1]
+                for c in range(chunks):
+                    r.bup_o[:, c * BLOCK:(c + 1) * BLOCK] = acc[12 + c:13 + c]
+            else:
+                r.bq_o[...] = acc[0:1]
+                r.bv_o[...] = acc[1:2]
+
+    r.acc[...] = r.gp[...]
+
+    def feed_back(j):
+        da = dot_nt(r.dlow[...], r.wd[j])
+        ug = (da * r.slope[j].astype(F32)).astype(BF)
+        for i in range(items):
+            r.upg[i, pl.ds(0, rows_pad), :] = ug[i * rows_pad:(i + 1) * rows_pad]
+        r.acc[...] += dot_nt(ug, r.wu[j])
+        down = dot_nn(r.dT[...], r.active[j].reshape(items * lanes, BLOCK))
+        up = dot_nn(r.hT[...], r.upg[...].reshape(items * lanes, BLOCK))
+        return down, up
+
+    def back_far(c, carry):
+        down, up = feed_back(chunks + c)
+        start_core(2 * c, down)
+        start_core(2 * c + 1, up[:width])
+        r.v_out[0, pl.ds(12 + c, 1), :] = up[width:width + 1]
+        return carry
+
+    lax.fori_loop(0, chunks, back_far, 0)
+
+    def back_own(half, carry):
+        for k in range(2):
+            c = 2 * half + k
+            down, up = feed_back(c)
+            start_a(2 * c, down, 2 * k)
+            start_a(2 * c + 1, up[:width], 2 * k + 1)
+            r.v_own[0, pl.ds(12 + c, 1), :] = up[width:width + 1]
+        return carry
+
+    lax.fori_loop(0, chunks // 2, back_own, 0)
+    start_b(0)
+    start_b(1)
+
+    def first_back(i, carry):
+        bout, gain1, shift1 = carry
+        hidden_grad = r.acc[rows_of(i), :]
+        normed = r.n1[rows_of(i), :]
+        inverse = r.inv1[rows_of(i), :][:, :1]
+        g = hidden_grad * r.gain_one[...]
+        grad = inverse * (
+            g - jnp.mean(g, axis=1, keepdims=True) - normed * jnp.mean(g * normed, axis=1, keepdims=True))
+        r.gp[rows_of(i), :] = grad
+        r.olow[i, pl.ds(0, rows_pad), :] = grad.astype(BF)
+        r.dT[:, lanes_of(i)] = transposed(grad)
+        return (bout + jnp.sum(grad, axis=0, keepdims=True),
+                gain1 + jnp.sum(hidden_grad * normed, axis=0, keepdims=True),
+                shift1 + jnp.sum(hidden_grad, axis=0, keepdims=True))
+
+    bout, gain1, shift1 = lax.fori_loop(0, items, first_back, (zero_vec, zero_vec, zero_vec))
+    for k, v in enumerate((bout, gain1, shift1, bdown, gain2, shift2)):
+        for part in range(2):
+            piece = v[:, part * BLOCK:(part + 1) * BLOCK]
+            r.v_out[0, pl.ds(2 * k + part, 1), :] = piece
+            r.v_own[0, pl.ds(2 * k + part, 1), :] = piece
+    vec_core(0).start()
+    start_b(2)
+    start_b(3)
+
+    start_core(8, dot_nt(r.dT[...], r.ctxT[1]))
+    out_grad = dot_nt(r.dT[...], r.ctxT[0])
+    for slot in range(2):
+        for i in range(items):
+            r.cgT[slot * items + i] = dot_nt(r.wo[slot], r.olow[i]).astype(BF)
+    start_a(8, out_grad, ORDER[8])
+    start_b(4)
+    start_b(5)
+
+    def attend_back(n):
+        i = lax.rem(n, items)
+        slot = n // items
+        for h in range(4):
+            pair = slice((h // 2) * 128, (h // 2) * 128 + 128)
+            head = slice(h * 64, (h + 1) * 64)
+            values = r.nat[n, 2, :, pair] * half[h % 2]
+            pg = dot_nn(values, r.cgT[n, pair, :])
+            p = r.probs[n * 4 + h, pl.ds(0, rows_pad), :].astype(F32)
+            inner = jnp.sum(p * pg, axis=0, keepdims=True)
+            r.dscore[h % 2, pl.ds(0, rows_pad), :] = (p * (pg - inner)).astype(BF)
+            ds = r.dscore[h % 2]
+            base = h * 64
+            r.gT[slot, pl.ds(base, 64), lanes_of(i)] = dot_nn(r.tra[n, 1, head, :], ds).astype(BF)
+            r.gT[slot, pl.ds(256 + base, 64), lanes_of(i)] = dot_nt(r.tra[n, 0, head, :], ds).astype(BF)
+            r.gT[slot, pl.ds(512 + base, 64), lanes_of(i)] = dot_nt(
+                r.cgT[n, head, :], r.probs[n * 4 + h]).astype(BF)
+
+    def projection_grad(slot, k):
+        return dot_nt(r.xT[...], r.gT[slot, pl.ds(k * 256, 256), :])
+
+    after = (
+        lambda: (start_b(6), start_b(7), start_c(0), start_c(1), vec_next(0, 0)),
+        lambda: (start_c(2), start_c(3), start_b(8), vec_next(0, 1)),
+        lambda: (start_c(4), start_c(5), vec_next(0, 2)),
+        lambda: (start_c(6), start_c(7), vec_next(0, 3)),
+        lambda: (start_c(8),),
+        lambda: None)
+
+    for n in range(2 * items):
+        attend_back((n + items) % (2 * items))
+        after[n]()
+        if n == items - 1:
+            for k in range(3):
+                grad = projection_grad(1, k)
+                start_core(9 + k, grad[:width])
+                if k == 0:
+                    r.v_out[1, pl.ds(0, 1), :] = grad[width:width + 1]
+                if k == 2:
+                    r.v_out[1, pl.ds(1, 1), :] = grad[width:width + 1]
+            vec_core(1).start()
+    for k in range(3):
+        grad = projection_grad(0, k)
+        start_a(9 + k, grad[:width], ORDER[9 + k])
+        if k == 0:
+            r.v_own[1, pl.ds(0, 1), :] = grad[width:width + 1]
+        if k == 2:
+            r.v_own[1, pl.ds(1, 1), :] = grad[width:width + 1]
+    vec_next(1, 0)
+
+    for i in range(items):
+        acc = None
+        for slot in range(2):
+            for k in range(3):
+                term = dot_nn(r.wqkv[slot, k], r.gT[slot, pl.ds(k * 256, 256), lanes_of(i)])
+                acc = term if acc is None else acc + term
+        r.ig_v[pl.ds(i * length, length), :] = acc.T[:length] + r.gp[pl.ds(i * rows_pad, length), :]
+    grad_copy = pltpu.make_async_copy(r.ig_v, r.ig_h, r.out_sem.at[1])
+    grad_copy.start()
+    for k in range(3):
+        start_b(9 + k)
+    vec_next(1, 1)
+    for c in range(chunks):
+        r.gd_o[:, c * BLOCK:(c + 1) * BLOCK] = finish(2 * c)
+        r.gu_o[:, c * BLOCK:(c + 1) * BLOCK] = finish(2 * c + 1)
+    r.go_o[...] = finish(8)
+    for k in range(3):
+        start_c(9 + k)
+    vec_next(1, 2)
+    r.gq_o[...] = finish(9)
+    r.gk_o[...] = finish(10)
+    r.gv_o[...] = finish(11)
+    vec_next(1, 3)
+
+    for s in remote:
+        s.wait_send()
+    for u in range(UNITS):
+        to_core(u).wait_send()
+    out_copy.wait()
+    grad_copy.wait()
+
+
+def hand_over(count, *refs):
+    held, sems = refs[2 * count:3 * count], refs[-1]
+    into = [pltpu.make_async_copy(refs[k], held[k], sems.at[0, k]) for k in range(count)]
+    out = [pltpu.make_async_copy(held[k], refs[count + k], sems.at[1, k]) for k in range(count)]
+    for c in into:
+        c.start()
+    for c, d in zip(into, out, strict=True):
+        c.wait()
+        d.start()
+    for d in out:
+        d.wait()
+
+
+def layer_by_items(
+    inputs, region_counts, w_query, b_query, w_key, w_value, b_value, w_out, b_out, gain_one, shift_one,
+    w_up, b_up, w_down, b_down, gain_two, shift_two, cotangent,
+):
+    total_rows, width = inputs.shape
+    item_count = region_counts.shape[0]
+    length = total_rows // item_count
+    items = item_count // 2
+    rows_pad = -(-length // ITEM_PAD) * ITEM_PAD
+    lanes = -(-length // 128) * 128
+    dp_size = lax.axis_size("dp")
+    nz = dp_size // 4
+    shard = width // dp_size
+    total = items * rows_pad
+    chunks = w_up.shape[1] // BLOCK
+    own_rows = items * length
+
+    two_chunks = 2 * chunks
+    hd = w_query.shape[1]
+    inner = [
+        ("x_raw", (total_rows, width), BF), ("x_v", (total, width), BF), ("cot_raw", (total_rows + 16, width), F32),
+        ("bias_q", (2, 1, BLOCK), F32), ("bias_v", (2, 1, BLOCK), F32), ("bias_u", (2, 1, chunks * BLOCK), F32),
+        ("b_out", (1, width), F32), ("gain_one", (1, width), F32), ("shift_one", (1, width), F32),
+        ("b_down", (1, width), F32), ("gain_two", (1, width), F32), ("shift_two", (1, width), F32),
+        ("wqkv", (2, 3, width, hd), BF), ("wo", (2, hd, width), BF),
+        ("wu", (two_chunks, width, BLOCK), BF), ("wd", (two_chunks, BLOCK, width), BF),
+        ("xT", (width + 16, items * lanes), BF), ("hT", (width + 16, items * lanes), BF),
+        ("dT", (width, items * lanes), BF),
+        ("nat", (2 * items, 3, rows_pad, hd), BF), ("tra", (2 * items, 3, hd, lanes), BF),
+        ("probs", (8 * items, lanes, lanes), BF), ("ctxT", (2, hd, items * lanes), BF),
+        ("ctx", (2, total, hd), BF), ("n1", (total, width), F32), ("inv1", (total, 128), F32),
+        ("hlow", (total, width), BF), ("slope", (two_chunks, total, BLOCK), BF),
+        ("active", (two_chunks, items, lanes, BLOCK), BF), ("acc", (total, width), F32),
+        ("out_f", (total, width), F32), ("out_v", (own_rows, width), BF), ("ig_v", (own_rows, width), F32), ("gp", (total, width), F32), ("dlow", (total, width), BF),
+        ("upg", (items, lanes, BLOCK), BF), ("olow", (items, lanes, width), BF),
+        ("cgT", (2 * items, hd, lanes), BF), ("dscore", (2, lanes, lanes), BF),
+        ("gT", (2, 3 * hd, items * lanes), BF),
+        ("g_out", (UNITS, width, BLOCK), BF), ("g_core", (UNITS, width, BLOCK), BF),
+        ("g", (UNITS, 16, shard, BLOCK), BF), ("g_a", (UNITS, 8, shard, BLOCK), BF),
+        ("g_b", (UNITS, 4, shard, BLOCK), BF), ("g_c", (UNITS, 3, shard, BLOCK), BF),
+        ("v_out", (2, 16, BLOCK), F32), ("v_own", (2, 16, BLOCK), F32),
+        ("v_in", (2, 2 + nz, 16, BLOCK), F32), ("v_sum", (2, 3, 16, BLOCK), F32),
+    ]
+    n_weights = 8 + chunks
+    sems = [
+        ("in_sem", (16 + chunks,)), ("w_send", (n_weights,)), ("w_recv", (n_weights,)), ("out_sem", (2,)),
+        ("core_send", (UNITS,)), ("core_recv", (UNITS,)), ("a_send", (UNITS,)), ("a_recv", (UNITS,)),
+        ("b_send", (UNITS,)), ("b_recv", (UNITS,)), ("c_send", (UNITS, 3)), ("c_recv", (UNITS, 3)),
+        ("v_send", (2, 2 + nz)), ("v_recv", (2, 2 + nz)),
+    ]
+    operands = [
+        ("counts", region_counts), ("x_h", inputs), ("cot_h", cotangent), ("wq_h", w_query), ("wk_h", w_key),
+        ("wv_h", w_value), ("wo_h", w_out), ("wu_h", w_up), ("wd_h", w_down.reshape(chunks, BLOCK, width)),
+        ("b_query_h", b_query[None]), ("b_value_h", b_value[None]), ("b_up_h", b_up[None]), ("b_out_h", b_out[None]),
+        ("gain_one_h", gain_one[None]), ("shift_one_h", shift_one[None]), ("b_down_h", b_down[None]),
+        ("gain_two_h", gain_two[None]), ("shift_two_h", shift_two[None]),
+    ]
+    hidden = chunks * BLOCK
+    results = [
+        ("out_h", (own_rows, width), BF, pl.ANY), ("ig_h", (own_rows, width), F32, pl.ANY),
+        ("gq_o", (shard, hd), F32, pltpu.VMEM), ("bq_o", (1, hd), F32, pltpu.VMEM),
+        ("gk_o", (shard, hd), F32, pltpu.VMEM), ("gv_o", (shard, hd), F32, pltpu.VMEM),
+        ("bv_o", (1, hd), F32, pltpu.VMEM), ("go_o", (shard, hd), F32, pltpu.VMEM),
+        ("bout_o", (1, width), F32, pltpu.VMEM), ("gain1_o", (1, width), F32, pltpu.VMEM),
+        ("shift1_o", (1, width), F32, pltpu.VMEM), ("gu_o", (shard, hidden), F32, pltpu.VMEM),
+        ("bup_o", (1, hidden), F32, pltpu.VMEM), ("gd_o", (shard, hidden), F32, pltpu.VMEM),
+        ("bdown_o", (1, width), F32, pltpu.VMEM), ("gain2_o", (1, width), F32, pltpu.VMEM),
+        ("shift2_o", (1, width), F32, pltpu.VMEM),
+    ]
+    names = [n for n, _ in operands] + [n for n, *_ in results] + [n for n, *_ in inner] + [n for n, _ in sems]
+    smem = pl.BlockSpec(memory_space=pltpu.SMEM)
+    shapes = [jax.ShapeDtypeStruct(s, d) for _, s, d, _ in results]
+    made = pl.pallas_call(
+        functools.partial(layer_kernel, (items, length, rows_pad, lanes, nz, shard), names),
+        out_shape=shapes,
+        in_specs=[smem] + [pl.BlockSpec(memory_space=pl.ANY)] * (len(operands) - 1),
+        out_specs=[pl.BlockSpec(memory_space=m) for *_, m in results],
+        scratch_shapes=[pltpu.VMEM(s, d) for _, s, d in inner] + [pltpu.SemaphoreType.DMA(s) for _, s in sems],
+        compiler_params=pltpu.CompilerParams(
+            collective_id=0, has_side_effects=True, vmem_limit_bytes=63 * 2**20),
+        name="layer",
+    )(*[v for _, v in operands])
+    count = len(shapes)
+    made = pl.pallas_call(
+        functools.partial(hand_over, count),
+        out_shape=shapes,
+        in_specs=[pl.BlockSpec(memory_space=pl.ANY)] * count,
+        out_specs=[pl.BlockSpec(memory_space=pl.ANY)] * count,
+        scratch_shapes=[pltpu.VMEM(s.shape, s.dtype) for s in shapes] + [pltpu.SemaphoreType.DMA((2, count))],
+        name="hand_over",
+    )(*made)
+    made = [v.reshape(-1) if v.shape[0] == 1 else v for v in made]
+    made[7], made[13] = made[7].T, made[13].T
+    return tuple(made)
+
+
 def solution(mesh):
     placed = (
         P("dp", None),
@@ -259,8 +900,20 @@
         P(),
         P("dp", None),
     )
+    dp_size, mp_size = mesh.shape["dp"], mesh.shape["mp"]
+
+    def body(*args):
+        width, hidden = args[0].shape[1], args[11].shape[1]
+        whole_items = mp_size == 2 and args[1].shape[0] % 2 == 0
+        even_shards = dp_size == 16 and width % (16 * dp_size) == 0
+        blocks = args[2].shape[1] == BLOCK and width == 2 * BLOCK and hidden == 4 * BLOCK
+        fits = args[0].shape[0] // args[1].shape[0] <= 256
+        if whole_items and even_shards and blocks and fits:
+            return layer_by_items(*args)
+        return per_device(*args)
+
     return jax.shard_map(
-        per_device,
+        body,
         mesh=mesh,
         in_specs=placed,
         out_specs=(

time: 687 us -> 90.5 us (0.13); the launches traced: 679 us -> 90.4 us
  waiting for transfers between devices: 412 us -> 0 us
  Pallas kernels: 0 us -> 89.5 us
  matrix products: 80.6 us -> 0 us
  blocking collectives: 79 us -> 0 us
  local copies, waits for them, and re-layouts: 55 us -> 0 us
  other arithmetic: 36.4 us -> 0 us
  between operations: 15.2 us -> 0.83 us
    unnamed x13 -> x0, waiting for transfers between devices: 179 us -> none
    reduce_scatter x3 -> x0, waiting for transfers between devices: 155 us -> none  [the longest x1 74.8 us: per_device(): lax.psum_scatter(grad_w_up.astype(jnp.bfloat16), 'dp', scatter_dimension=...]
    pallas_call x0 -> x2, Pallas kernels: none -> 89.5 us  [the longest x1 86.4 us: layer_by_items(): pl.pallas_call(functools.partial(layer_kernel, (items, length, rows_pad,...]
    dot_general x24 -> x0, matrix products: 80.6 us -> none  [the longest x6 22.3 us: contract_rows(): lax.dot_general(first_op, second_op, (((0,), (0,)), ((), ())), preferred_...]
    psum x2 -> x0, blocking collectives: 79 us -> none  [the longest x1 40.7 us: per_device(): lax.psum((grad_b_out, grad_gain_one, grad_shift_one, grad_b_down, grad_ga...]
    psum x4 -> x0, waiting for transfers between devices: 78.6 us -> none  [the longest x1 25.2 us: per_device(): attended = lax.psum(partial_attn, 'mp')]
    reshape x11 -> x0, local copies, waits for them, and re-layouts: 26.6 us -> none  [the longest x8 18.3 us: split_heads(): return flat_rows.reshape(item_count, length, heads_here, HEAD_DIM)]
    reduce_sum x11 -> x0, other arithmetic: 23.2 us -> none  [the longest x2 5.61 us: layer_stats(): row_mean = jnp.mean(pre_rows, axis=-1, keepdims=True)]
  transfers between devices with their start and end apart: 10 -> 0, of which waited for: 10 -> 0; matrix products, arithmetic and copies ran while one was open for 14% -> 0% of each run, Pallas kernels for 0% -> 0%
where the time goes in v1:
time: 90.5 us; the launch traced here: 90.4 us
  Pallas kernels  89.5 us (99%)
    pallas_call x1, Pallas kernels, layer_by_items(): pl.pallas_call(functools.partial(layer_kernel, (items, length, rows_pad,...  86.4 us
    pallas_call x1, Pallas kernels, layer_by_items(): pl.pallas_call(functools.partial(hand_over, count), out_shape=shapes, in_...  3.14 us

profile of v1, /device:TPU:0, one launch (start us, length us, event | category | flops | bytes accessed | tf_op | source)
XLA Modules:
  0.0 90.4 jit_solution(9523934741969762224)
XLA Ops:
  0.7 86.4 %layer.1 = (bf16[684,512]{1,0:T(8,128)(2,1)}, f32[684,512]{1,0:T(8,128)}, f32[32,256]{1,0:T(8,128)}, f32[1,256]{1,0:T(1,128)}, f32[32,256]{1,0:T(8,128)}, /*inde...) custom-call(s32[6]{0:T(128)} %refs_0_.1, ...), custom_call_target="tpu_custom_call" | custom-call | tf_op jit(solution)/shard_map/layer/pallas_call | solution.py:858
  87.1 3.1 %hand_over.1 = (bf16[684,512]{1,0:T(8,128)(2,1)}, f32[684,512]{1,0:T(8,128)}, f32[32,256]{1,0:T(8,128)}, f32[1,256]{1,0:T(1,128)}, f32[32,256]{1,0:T(8,128)}, /*...) custom-call(bf16[684,512]{1,0:T(8,128)(2,1)} %get-tuple-element.51.r, ...), custom_call_target="tpu_custom_call" | custom-call | tf_op jit(solution)/shard_map/hand_over/pallas_call | solution.py:869

commit v2 on v1

--- a/solution.py
+++ b/solution.py
@@ -249,8 +249,8 @@
 F32 = jnp.float32
 BLOCK = 256
 UNITS = 12
-X_FIRST, Y_FIRST, LOW_FIRST, HIGH_FIRST = 0, 1, 2, 3
-ORDER = (0, 1, 2, 3, 0, 1, 2, 3, 0, 1, 2, 3)
+X_FIRST, Y_FIRST, Z_FIRST = 0, 1, 2
+ORDER = (0, 1, 2, 0, 1, 2, 0, 1, 1, 1, 2, 0)
 
 
 def dot_nn(a, b):
@@ -278,7 +278,7 @@
     y_side = (at(z, 1 - y, x), mp)
     z_side = [(at((z + step) % nz, y, x), mp) for step in range(1, nz)]
     low_side = (at(z + 1 - 2 * (z % 2), y, x), mp)
-    high_side = (at(nz - 1 - z, y, x), mp)
+    high_side = z_side[1]
     plane_side = [(at(z, (y + step // 2) % 2, (x + step) % 2), mp) for step in range(1, 4)]
 
     local = []
@@ -299,8 +299,10 @@
     c_wo = bring(r.wo_h, r.wo.at[0])
     c_wu = [bring(r.wu_h.at[:, pl.ds(c * BLOCK, BLOCK)], r.wu.at[c]) for c in range(chunks)]
     c_wd = bring(r.wd_h, r.wd.at[pl.ds(0, chunks)])
-    full_rows = r.cot_h.shape[0]
-    c_cot = bring(r.cot_h, r.cot_raw.at[pl.ds(0, full_rows)])
+    full_rows = r.x_h.shape[0]
+    base = items * length // 8 * 8
+    cot_count = full_rows - base
+    c_cot = bring(r.cot_h.at[pl.ds(pl.multiple_of(mp * base, 8), cot_count)], r.cot_raw.at[pl.ds(0, cot_count)])
 
     barrier = pltpu.get_barrier_semaphore()
     near = [core] + plane_side + z_side
@@ -345,18 +347,18 @@
     lax.fori_loop(0, r.probs.shape[0], clear, 0)
     zero_block = jnp.zeros((pad_rows, BLOCK), BF)
     for i in range(items):
-        r.upg[i, pl.ds(rows_pad, pad_rows), :] = zero_block
-        r.olow[i, pl.ds(rows_pad, pad_rows), :] = jnp.zeros((pad_rows, r.olow.shape[2]), BF)
+        r.olow[i, pl.ds(rows_pad, pad_rows), :] = jnp.zeros((pad_rows, width), BF)
+        for j in range(r.upg.shape[0]):
+            r.upg[j, i, pl.ds(rows_pad, pad_rows), :] = zero_block
         for j in range(2 * chunks):
             r.active[j, i, pl.ds(rows_pad, pad_rows), :] = zero_block
-    for k in range(2):
+    for k in range(r.dscore.shape[0]):
         r.dscore[k, pl.ds(rows_pad, pad_rows), :] = jnp.zeros((pad_rows, lanes), BF)
     one_row = jnp.where(lax.broadcasted_iota(jnp.int32, (16, items * lanes), 0) == 0, 1.0, 0.0).astype(BF)
     r.xT[pl.ds(width, 16), :] = one_row
     r.hT[pl.ds(width, 16), :] = one_row
-
     cot_rows = r.cot_raw.shape[0]
-    r.cot_raw[pl.ds(full_rows, cot_rows - full_rows), :] = jnp.zeros((cot_rows - full_rows, width), F32)
+    r.cot_raw[pl.ds(cot_count, cot_rows - cot_count), :] = jnp.zeros((cot_rows - cot_count, width), F32)
 
     c_x.wait()
     down_ = lax.broadcasted_iota(jnp.int32, (rows_pad, 256), 0)
@@ -372,146 +374,182 @@
             term = dot_nn(pick[:, :count], r.x_raw[pl.ds(window, count), :])
             block = term if block is None else block + term
         r.x_v[rows_of(i), :] = block.astype(BF)
-        r.xT[pl.ds(0, width), lanes_of(i)] = transposed(block)
-
-    def project(slot):
-        def one(k, carry):
-            shift = jnp.where(k == 0, r.bias_q[slot], jnp.where(k == 2, r.bias_v[slot], 0.0))
-            acc = dot_nn(r.x_v[...], r.wqkv[slot, k]) + shift
-            for i in range(items):
-                block = acc[i * rows_pad:(i + 1) * rows_pad]
-                r.nat[slot * items + i, k] = block.astype(BF)
-                low = block.astype(BF).astype(F32)
-                r.tra[slot * items + i, k] = transposed(low * jnp.where(k == 2, 1.0, 0.125))
-            return carry
-
-        lax.fori_loop(0, 3, one, 0)
+
+    def project(slot, k):
+        r.work[k] = dot_nn(r.x_v[...], r.wqkv[slot, k])
+
+    def keep(slot, k):
+        for i in range(items):
+            block = r.work[k, pl.ds(i * rows_pad, rows_pad), :]
+            n = slot * items + i
+            if k == 0:
+                r.tra[n, 0] = transposed((block + r.bias_q[slot]) * 0.125)
+            elif k == 1:
+                r.keys[n] = block.astype(BF)
+            else:
+                block = block + r.bias_v[slot]
+                r.values[n] = block.astype(BF)
+                r.tra[n, 2] = transposed(block)
 
     for c in c_w + c_p:
         c.wait()
-    project(0)
-    for s in s_w:
-        s.wait_recv()
-    project(1)
+    for k in range(3):
+        project(0, k)
+    for k in range(3):
+        keep(0, k)
+    for c in s_w:
+        c.wait_recv()
+    for k in range(3):
+        project(1, k)
 
     lane = lax.broadcasted_iota(jnp.int32, (1, 128), 1)
     half = [jnp.where(lane < 64, 1.0, 0.0).astype(BF), jnp.where(lane >= 64, 1.0, 0.0).astype(BF)]
-
     position = lax.broadcasted_iota(jnp.int32, (rows_pad, lanes), 0)
 
-    def attend(n, carry):
-        i = lax.rem(n, items)
-        mask = jnp.where(position < TEXT + r.counts[mp * items + i], 0.0, -1e9)
-        parts = []
+    def pair_of(h):
+        return slice((h // 2) * 128, (h // 2) * 128 + 128)
+
+    def head_of(h):
+        return slice(h * 64, (h + 1) * 64)
+
+    def scores_of(n):
         for h in range(4):
-            pair = slice((h // 2) * 128, (h // 2) * 128 + 128)
-            keys = r.nat[n, 1, :, pair] * half[h % 2]
-            score = dot_nn(keys, r.tra[n, 0, pair, :]) + mask
+            r.score[(n % 2) * 4 + h] = dot_nn(r.keys[n, :, pair_of(h)] * half[h % 2], r.tra[n, 0, pair_of(h), :])
+
+    def soften(n):
+        mask = jnp.where(position < TEXT + r.counts[mp * items + n % items], 0.0, -1e9)
+        for h in range(4):
+            score = r.score[(n % 2) * 4 + h] + mask
             top = jnp.max(score, axis=0, keepdims=True)
             e = jnp.exp(score - top)
             p = e * (1.0 / jnp.sum(e, axis=0, keepdims=True))
             r.probs[n * 4 + h, pl.ds(0, rows_pad), :] = p.astype(BF)
-            parts.append(dot_nn(r.tra[n, 2, h * 64:(h + 1) * 64, :], r.probs[n * 4 + h]))
+
+    def contexts_of(n):
+        parts = [dot_nn(r.tra[n, 2, head_of(h), :], r.probs[n * 4 + h]) for h in range(4)]
         context = jnp.concatenate(parts, axis=0)
-        slot = n // items
-        r.ctxT[slot, :, lanes_of(i)] = context.astype(BF)
-        r.ctx[slot, rows_of(i), :] = context.T[:rows_pad].astype(BF)
-        return carry
-
-    lax.fori_loop(0, 2 * items, attend, 0)
+        slot, i = n // items, n % items
+        r.ctxT[slot, :, pl.ds(i * lanes, lanes)] = context.astype(BF)
+        r.ctx[slot, pl.ds(i * rows_pad, rows_pad), :] = context.T[:rows_pad].astype(BF)
+
+    scores_of(0)
+    for n in range(2 * items):
+        if n + 1 < 2 * items:
+            if n + 1 == items:
+                for k in range(3):
+                    keep(1, k)
+            scores_of(n + 1)
+        soften(n)
+        contexts_of(n)
 
     c_wo.wait()
     s_wo.wait_recv()
     for c in c_vec:
         c.wait()
 
-    def first_norm(i, carry):
-        att = dot_nn(r.ctx[0, rows_of(i), :], r.wo[0]) + dot_nn(r.ctx[1, rows_of(i), :], r.wo[1])
-        pre = att + r.b_out[...] + r.x_v[rows_of(i), :].astype(F32)
+    def attended(i):
+        rows = pl.ds(i * rows_pad, rows_pad)
+        r.acc[rows, :] = dot_nn(r.ctx[0, rows, :], r.wo[0]) + dot_nn(r.ctx[1, rows, :], r.wo[1])
+
+    def first_norm(i):
+        rows = pl.ds(i * rows_pad, rows_pad)
+        pre = r.acc[rows, :] + r.b_out[...] + r.x_v[rows, :].astype(F32)
         centred = pre - jnp.mean(pre, axis=1, keepdims=True)
         inverse = lax.rsqrt(jnp.mean(centred * centred, axis=1, keepdims=True) + 1e-12)
         normed = centred * inverse
-        r.n1[rows_of(i), :] = normed
-        r.inv1[rows_of(i), :] = jnp.broadcast_to(inverse, (rows_pad, 128))
-        hidden = normed * r.gain_one[...] + r.shift_one[...]
-        r.hlow[rows_of(i), :] = hidden.astype(BF)
-        r.hT[pl.ds(0, width), lanes_of(i)] = transposed(hidden)
-        return carry
-
-    lax.fori_loop(0, items, first_norm, 0)
+        r.n1[rows, :] = normed
+        r.inv1[rows, :] = jnp.broadcast_to(inverse, (rows_pad, 128))
+        r.hlow[rows, :] = (normed * r.gain_one[...] + r.shift_one[...]).astype(BF)
+
+    for i in range(items):
+        attended(i)
+    for i in range(items):
+        first_norm(i)
 
     for c in c_wu + [c_wd]:
         c.wait()
-    for s in s_wu + [s_wd]:
-        s.wait_recv()
-    r.acc[...] = jnp.zeros(r.acc.shape, F32)
-
-    def feed(j, carry):
-        slot, c = j // chunks, lax.rem(j, chunks)
-        up_bias = r.bias_u[slot, :, pl.ds(pl.multiple_of(c * BLOCK, BLOCK), BLOCK)]
+    for c in s_wu + [s_wd]:
+        c.wait_recv()
+    c_cot.wait()
+    valid = lax.broadcasted_iota(jnp.int32, (rows_pad, 1), 0) < length
+
+    def own_cotangent(i):
+        at_ = [r.cot_raw[pl.ds(m * (items * length - base) + i * length, rows_pad), :] for m in range(2)]
+        r.cot[pl.ds(i * rows_pad, rows_pad), :] = jnp.where(valid, jnp.where(mp == 0, at_[0], at_[1]), 0.0)
+
+    def lift(j):
+        slot, c = j // chunks, j % chunks
+        r.work[j % 2] = dot_nn(r.hlow[...], r.wu[j]) + r.bias_u[slot, :, c * BLOCK:(c + 1) * BLOCK]
+
+    def activate(j):
         for i in range(items):
-            u = dot_nn(r.hlow[rows_of(i), :], r.wu[j]) + up_bias
+            rows = pl.ds(i * rows_pad, rows_pad)
+            u = r.work[j % 2, rows, :]
             phi = 0.5 + 0.5 * lax.erf(u * 0.7071067811865476)
-            r.slope[j, rows_of(i), :] = (phi + u * (jnp.exp(-0.5 * u * u) * 0.3989422804014327)).astype(BF)
-            act = (u * phi).astype(BF)
-            r.active[j, i, pl.ds(0, rows_pad), :] = act
-            r.acc[rows_of(i), :] += dot_nn(act, r.wd[j])
-        return carry
-
-    lax.fori_loop(0, 2 * chunks, feed, 0)
-
-    c_cot.wait()
-    sums = [None, None, None]
-
-    valid = lax.broadcasted_iota(jnp.int32, (rows_pad, 1), 0) < length
-
-    def second_norm(i, carry):
-        gain2, shift2, bdown = carry
-        hidden = r.n1[rows_of(i), :] * r.gain_one[...] + r.shift_one[...]
-        pre = r.acc[rows_of(i), :] + r.b_down[...] + hidden
-        centred = pre - jnp.mean(pre, axis=1, keepdims=True)
-        inverse = lax.rsqrt(jnp.mean(centred * centred, axis=1, keepdims=True) + 1e-12)
+            r.slope[j, rows, :] = (phi + u * (jnp.exp(-0.5 * u * u) * 0.3989422804014327)).astype(BF)
+            r.active[j, i, pl.ds(0, rows_pad), :] = (u * phi).astype(BF)
+
+    def lower(j):
+        part = dot_nn(r.active[j][:, :rows_pad].reshape(total, BLOCK), r.wd[j])
+        if j == 0:
+            r.acc[...] = part
+        else:
+            r.acc[...] += part
+
+    lift(0)
+    for j in range(2 * chunks):
+        if j > 0:
+            lower(j - 1)
+        if j + 1 < 2 * chunks:
+            lift(j + 1)
+        activate(j)
+        if 2 <= j < 2 + items:
+            own_cotangent(j - 2)
+    lower(2 * chunks - 1)
+
+    def mean(v):
+        return jnp.mean(v, axis=1, keepdims=True)
+
+    def column_sum(v):
+        return jnp.sum(v, axis=0, keepdims=True)
+
+    gain2, shift2, bdown = [], [], []
+
+    def second_norm(i):
+        rows = pl.ds(i * rows_pad, rows_pad)
+        hidden = r.n1[rows, :] * r.gain_one[...] + r.shift_one[...]
+        pre = r.acc[rows, :] + r.b_down[...] + hidden
+        centred = pre - mean(pre)
+        inverse = lax.rsqrt(mean(centred * centred) + 1e-12)
         normed = centred * inverse
-        r.out_f[pl.ds(i * length, rows_pad), :] = normed * r.gain_two[...] + r.shift_two[...]
-        pieces = [r.cot_raw[pl.ds((m * items + i) * length, rows_pad), :] for m in range(2)]
-        cot = jnp.where(valid, jnp.where(mp == 0, pieces[0], pieces[1]), 0.0)
+        cot = r.cot[rows, :]
         g = cot * r.gain_two[...]
-        grad = inverse * (
-            g - jnp.mean(g, axis=1, keepdims=True) - normed * jnp.mean(g * normed, axis=1, keepdims=True))
-        r.gp[rows_of(i), :] = grad
-        r.dlow[rows_of(i), :] = grad.astype(BF)
-        r.dT[:, lanes_of(i)] = transposed(grad)
-        return (gain2 + jnp.sum(cot * normed, axis=0, keepdims=True),
-                shift2 + jnp.sum(cot, axis=0, keepdims=True),
-                bdown + jnp.sum(grad, axis=0, keepdims=True))
-
-    zero_vec = jnp.zeros((1, width), F32)
-    carry = (zero_vec, zero_vec, zero_vec)
+        grad = inverse * (g - mean(g) - normed * mean(g * normed))
+        r.gp[rows, :] = grad
+        r.dlow[rows, :] = grad.astype(BF)
+        r.dT[:, pl.ds(i * lanes, lanes)] = transposed(grad)
+        r.acc[pl.ds(i * length, rows_pad), :] = normed * r.gain_two[...] + r.shift_two[...]
+        gain2.append(column_sum(cot * normed))
+        shift2.append(column_sum(cot))
+        bdown.append(column_sum(grad))
+
     for i in range(items):
-        carry = second_norm(i, carry)
-    gain2, shift2, bdown = carry
-    r.out_v[...] = r.out_f[pl.ds(0, items * length), :].astype(BF)
-    out_copy = pltpu.make_async_copy(r.out_v, r.out_h, r.out_sem.at[0])
-    out_copy.start()
+        second_norm(i)
 
     def to_core(u):
         return pltpu.make_async_remote_copy(
-            src_ref=r.g_out.at[u], dst_ref=r.g_core.at[u], send_sem=r.core_send.at[u],
+            src_ref=r.g_out.at[u], dst_ref=r.g.at[u], send_sem=r.core_send.at[u],
             recv_sem=r.core_recv.at[u], device_id=core, device_id_type=MESH)
 
-    place_z = jnp.where(z == 0, 0, jnp.where(z == nz - 1, 1, z + 1))
     route = (
-        (x, y, z, x_side, y_side), (y, x, z, y_side, x_side),
-        (place_z // 2, place_z % 2, y * 2 + x, low_side, high_side), (z // 2, z % 2, y * 2 + x, high_side, low_side))
-    shards = 4 * nz
+        (x, y, z, x_side, y_side), (y, x, z, y_side, x_side), (z % 2, z // 2, y * 2 + x, low_side, high_side))
 
     def shard_order(order):
         if order == X_FIRST:
             return [at(c, b, a) for a in range(2) for b in range(2) for c in range(nz)]
         if order == Y_FIRST:
             return [at(c, a, b) for a in range(2) for b in range(2) for c in range(nz)]
-        ring = (0, nz - 1, 1, 2) if order == LOW_FIRST else (0, 1, 2, 3)
-        return [at(c, b, a) for c in ring for b in range(2) for a in range(2)]
+        return [at(2 * b + a, c, d) for a in range(2) for b in range(2) for c in range(2) for d in range(2)]
 
     def stage_a(u, order):
         first, _, _, device, _ = route[order]
@@ -537,15 +575,19 @@
             device_id=device, device_id_type=MESH)
 
     def start_core(u, value):
-        r.g_out[u] = value.astype(BF)
+        for place, block in enumerate(shard_order(ORDER[u])):
+            r.g_out[u, place] = value[block * shard:(block + 1) * shard].astype(BF)
         to_core(u).start()
 
-    def start_a(u, value, order):
+    def hold(u, value):
+        r.own[u % r.own.shape[0]] = value
+
+    def start_a(u):
         to_core(u).wait_recv()
-        total_ = (value + r.g_core[u].astype(F32)).astype(BF)
-        for place, block in enumerate(shard_order(order)):
-            r.g[u, place] = total_[block * shard:(block + 1) * shard]
-        stage_a(u, order).start()
+        for place, block in enumerate(shard_order(ORDER[u])):
+            mine = r.own[u % r.own.shape[0], pl.ds(block * shard, shard), :]
+            r.g[u, place] = (mine + r.g[u, place].astype(F32)).astype(BF)
+        stage_a(u, ORDER[u]).start()
 
     def start_b(u):
         order = ORDER[u]
@@ -620,143 +662,182 @@
                 r.bq_o[...] = acc[0:1]
                 r.bv_o[...] = acc[1:2]
 
-    r.acc[...] = r.gp[...]
-
-    def feed_back(j):
-        da = dot_nt(r.dlow[...], r.wd[j])
-        ug = (da * r.slope[j].astype(F32)).astype(BF)
+    def down_grad(j):
+        return dot_nn(r.dT[...], r.active[j].reshape(items * lanes, BLOCK))
+
+    def active_grad(j):
+        r.work[j % 2] = dot_nt(r.dlow[...], r.wd[j])
+
+    def upper_grad(j):
         for i in range(items):
-            r.upg[i, pl.ds(0, rows_pad), :] = ug[i * rows_pad:(i + 1) * rows_pad]
-        r.acc[...] += dot_nt(ug, r.wu[j])
-        down = dot_nn(r.dT[...], r.active[j].reshape(items * lanes, BLOCK))
-        up = dot_nn(r.hT[...], r.upg[...].reshape(items * lanes, BLOCK))
-        return down, up
-
-    def back_far(c, carry):
-        down, up = feed_back(chunks + c)
-        start_core(2 * c, down)
-        start_core(2 * c + 1, up[:width])
-        r.v_out[0, pl.ds(12 + c, 1), :] = up[width:width + 1]
-        return carry
-
-    lax.fori_loop(0, chunks, back_far, 0)
-
-    def back_own(half, carry):
-        for k in range(2):
-            c = 2 * half + k
-            down, up = feed_back(c)
-            start_a(2 * c, down, 2 * k)
-            start_a(2 * c + 1, up[:width], 2 * k + 1)
+            rows = pl.ds(i * rows_pad, rows_pad)
+            r.upg[j % 3, i, pl.ds(0, rows_pad), :] = (r.work[j % 2, rows, :] * r.slope[j, rows, :].astype(F32)).astype(BF)
+
+    def up_grad(j):
+        return dot_nn(r.hT[...], r.upg[j % 3].reshape(items * lanes, BLOCK))
+
+    def hidden_grad(j):
+        r.gp[...] += dot_nt(r.upg[j % 3][:, :rows_pad].reshape(total, BLOCK), r.wu[j])
+
+    def turn(i):
+        rows = pl.ds(i * rows_pad, rows_pad)
+        r.hT[pl.ds(0, width), pl.ds(i * lanes, lanes)] = transposed(r.hlow[rows, :].astype(F32))
+
+    def turn_input(i):
+        rows = pl.ds(i * rows_pad, rows_pad)
+        r.xT[pl.ds(0, width), pl.ds(i * lanes, lanes)] = transposed(r.x_v[rows, :].astype(F32))
+
+    def turn_keys(n):
+        r.tra[n, 1] = transposed(r.keys[n].astype(F32) * 0.125)
+
+    for c in range(chunks):
+        start_core(c, down_grad(chunks + c))
+    for c in range(chunks):
+        hold(c, down_grad(c))
+        if c < items:
+            turn(c)
+    r.out_v[...] = r.acc[pl.ds(0, items * length), :].astype(BF)
+    out_copy = pltpu.make_async_copy(r.out_v, r.out_h, r.out_sem.at[0])
+    out_copy.start()
+    order = list(range(chunks, 2 * chunks)) + list(range(chunks))
+    active_grad(order[0])
+    for c in range(chunks):
+        start_a(c)
+    for k, j in enumerate(order):
+        if k + 1 < 2 * chunks:
+            active_grad(order[k + 1])
+        upper_grad(j)
+        up = up_grad(j)
+        c = j % chunks
+        if j >= chunks:
+            start_core(chunks + c, up)
+            r.v_out[0, pl.ds(12 + c, 1), :] = up[width:width + 1]
+        else:
+            hold(chunks + c, up[:width])
             r.v_own[0, pl.ds(12 + c, 1), :] = up[width:width + 1]
-        return carry
-
-    lax.fori_loop(0, chunks // 2, back_own, 0)
-    start_b(0)
-    start_b(1)
-
-    def first_back(i, carry):
-        bout, gain1, shift1 = carry
-        hidden_grad = r.acc[rows_of(i), :]
-        normed = r.n1[rows_of(i), :]
-        inverse = r.inv1[rows_of(i), :][:, :1]
-        g = hidden_grad * r.gain_one[...]
-        grad = inverse * (
-            g - jnp.mean(g, axis=1, keepdims=True) - normed * jnp.mean(g * normed, axis=1, keepdims=True))
-        r.gp[rows_of(i), :] = grad
+        hidden_grad(j)
+        if k < 2 * items:
+            turn_keys(k)
+        else:
+            turn_input(k - 2 * items)
+        if j < chunks:
+            start_a(chunks + c)
+    turn_input(2)
+    for u in range(3):
+        start_b(u)
+
+    bout, gain1, shift1 = [], [], []
+
+    def first_back(i):
+        rows = pl.ds(i * rows_pad, rows_pad)
+        hidden = r.gp[rows, :]
+        normed = r.n1[rows, :]
+        inverse = r.inv1[rows, :][:, :1]
+        g = hidden * r.gain_one[...]
+        grad = inverse * (g - mean(g) - normed * mean(g * normed))
+        r.gp[rows, :] = grad
         r.olow[i, pl.ds(0, rows_pad), :] = grad.astype(BF)
-        r.dT[:, lanes_of(i)] = transposed(grad)
-        return (bout + jnp.sum(grad, axis=0, keepdims=True),
-                gain1 + jnp.sum(hidden_grad * normed, axis=0, keepdims=True),
-                shift1 + jnp.sum(hidden_grad, axis=0, keepdims=True))
-
-    bout, gain1, shift1 = lax.fori_loop(0, items, first_back, (zero_vec, zero_vec, zero_vec))
+        r.oT[:, pl.ds(i * lanes, lanes)] = transposed(grad)
+        bout.append(column_sum(grad))
+        gain1.append(column_sum(hidden * normed))
+        shift1.append(column_sum(hidden))
+
+    for i in range(items):
+        first_back(i)
     for k, v in enumerate((bout, gain1, shift1, bdown, gain2, shift2)):
+        v = sum(v[1:], v[0])
         for part in range(2):
             piece = v[:, part * BLOCK:(part + 1) * BLOCK]
             r.v_out[0, pl.ds(2 * k + part, 1), :] = piece
             r.v_own[0, pl.ds(2 * k + part, 1), :] = piece
     vec_core(0).start()
-    start_b(2)
-    start_b(3)
-
-    start_core(8, dot_nt(r.dT[...], r.ctxT[1]))
-    out_grad = dot_nt(r.dT[...], r.ctxT[0])
-    for slot in range(2):
-        for i in range(items):
-            r.cgT[slot * items + i] = dot_nt(r.wo[slot], r.olow[i]).astype(BF)
-    start_a(8, out_grad, ORDER[8])
-    start_b(4)
-    start_b(5)
-
-    def attend_back(n):
-        i = lax.rem(n, items)
-        slot = n // items
+
+    start_core(8, dot_nt(r.oT[...], r.ctxT[1]))
+    for n in [*range(items, 2 * items), *range(items)]:
+        r.cgT[n] = dot_nt(r.wo[n // items], r.olow[n % items]).astype(BF)
+    hold(8, dot_nt(r.oT[...], r.ctxT[0]))
+
+    def probs_grad(n):
         for h in range(4):
-            pair = slice((h // 2) * 128, (h // 2) * 128 + 128)
-            head = slice(h * 64, (h + 1) * 64)
-            values = r.nat[n, 2, :, pair] * half[h % 2]
-            pg = dot_nn(values, r.cgT[n, pair, :])
+            r.score[(n % 2) * 4 + h] = dot_nn(r.values[n, :, pair_of(h)] * half[h % 2], r.cgT[n, pair_of(h), :])
+
+    def store_grad(n, k, h, value):
+        r.gT[n // items, pl.ds(k * 256 + h * 64, 64), pl.ds((n % items) * lanes, lanes)] = value.astype(BF)
+
+    def value_grad(n):
+        for h in range(4):
+            store_grad(n, 2, h, dot_nt(r.cgT[n, head_of(h), :], r.probs[n * 4 + h]))
+
+    def score_grad(n):
+        for h in range(4):
+            pg = r.score[(n % 2) * 4 + h]
             p = r.probs[n * 4 + h, pl.ds(0, rows_pad), :].astype(F32)
             inner = jnp.sum(p * pg, axis=0, keepdims=True)
-            r.dscore[h % 2, pl.ds(0, rows_pad), :] = (p * (pg - inner)).astype(BF)
-            ds = r.dscore[h % 2]
-            base = h * 64
-            r.gT[slot, pl.ds(base, 64), lanes_of(i)] = dot_nn(r.tra[n, 1, head, :], ds).astype(BF)
-            r.gT[slot, pl.ds(256 + base, 64), lanes_of(i)] = dot_nt(r.tra[n, 0, head, :], ds).astype(BF)
-            r.gT[slot, pl.ds(512 + base, 64), lanes_of(i)] = dot_nt(
-                r.cgT[n, head, :], r.probs[n * 4 + h]).astype(BF)
+            r.dscore[(n % 2) * 4 + h, pl.ds(0, rows_pad), :] = (p * (pg - inner)).astype(BF)
+
+    def query_key_grad(n):
+        for h in range(4):
+            ds = r.dscore[(n % 2) * 4 + h]
+            store_grad(n, 0, h, dot_nn(r.tra[n, 1, head_of(h), :], ds))
+            store_grad(n, 1, h, dot_nt(r.tra[n, 0, head_of(h), :], ds))
 
     def projection_grad(slot, k):
         return dot_nt(r.xT[...], r.gT[slot, pl.ds(k * 256, 256), :])
 
     after = (
-        lambda: (start_b(6), start_b(7), start_c(0), start_c(1), vec_next(0, 0)),
-        lambda: (start_c(2), start_c(3), start_b(8), vec_next(0, 1)),
-        lambda: (start_c(4), start_c(5), vec_next(0, 2)),
-        lambda: (start_c(6), start_c(7), vec_next(0, 3)),
-        lambda: (start_c(8),),
-        lambda: None)
-
-    for n in range(2 * items):
-        attend_back((n + items) % (2 * items))
-        after[n]()
-        if n == items - 1:
-            for k in range(3):
-                grad = projection_grad(1, k)
-                start_core(9 + k, grad[:width])
-                if k == 0:
-                    r.v_out[1, pl.ds(0, 1), :] = grad[width:width + 1]
-                if k == 2:
-                    r.v_out[1, pl.ds(1, 1), :] = grad[width:width + 1]
+        lambda: (start_a(8), vec_next(0, 0)),
+        lambda: start_b(3),
+        lambda: (start_c(0), start_c(1), start_c(2), vec_next(0, 1)),
+        lambda: (start_b(4), start_b(5)),
+        lambda: (start_b(6), start_c(3)),
+        lambda: (start_b(7), start_c(4), vec_next(0, 2)))
+    for k in range(2 * items):
+        n = (k + items) % (2 * items)
+        probs_grad(n)
+        value_grad(n)
+        score_grad(n)
+        query_key_grad(n)
+        if k == items - 1:
+            for part in range(3):
+                grad = projection_grad(1, part)
+                start_core(9 + part, grad)
+                if part != 1:
+                    r.v_out[1, pl.ds(part // 2, 1), :] = grad[width:width + 1]
             vec_core(1).start()
-    for k in range(3):
-        grad = projection_grad(0, k)
-        start_a(9 + k, grad[:width], ORDER[9 + k])
-        if k == 0:
-            r.v_own[1, pl.ds(0, 1), :] = grad[width:width + 1]
-        if k == 2:
-            r.v_own[1, pl.ds(1, 1), :] = grad[width:width + 1]
+        after[k]()
+    for part in range(3):
+        grad = projection_grad(0, part)
+        hold(9 + part, grad[:width])
+        if part != 1:
+            r.v_own[1, pl.ds(part // 2, 1), :] = grad[width:width + 1]
+        start_a(9 + part)
     vec_next(1, 0)
 
     for i in range(items):
         acc = None
         for slot in range(2):
             for k in range(3):
-                term = dot_nn(r.wqkv[slot, k], r.gT[slot, pl.ds(k * 256, 256), lanes_of(i)])
+                term = dot_nn(r.wqkv[slot, k], r.gT[slot, pl.ds(k * 256, 256), pl.ds(i * lanes, lanes)])
                 acc = term if acc is None else acc + term
         r.ig_v[pl.ds(i * length, length), :] = acc.T[:length] + r.gp[pl.ds(i * rows_pad, length), :]
     grad_copy = pltpu.make_async_copy(r.ig_v, r.ig_h, r.out_sem.at[1])
     grad_copy.start()
+    start_b(8)
+    start_c(5)
+    start_c(6)
+    start_c(7)
     for k in range(3):
         start_b(9 + k)
     vec_next(1, 1)
+    start_c(8)
+    vec_next(0, 3)
     for c in range(chunks):
-        r.gd_o[:, c * BLOCK:(c + 1) * BLOCK] = finish(2 * c)
-        r.gu_o[:, c * BLOCK:(c + 1) * BLOCK] = finish(2 * c + 1)
-    r.go_o[...] = finish(8)
+        r.gd_o[:, c * BLOCK:(c + 1) * BLOCK] = finish(c)
+        r.gu_o[:, c * BLOCK:(c + 1) * BLOCK] = finish(chunks + c)
     for k in range(3):
         start_c(9 + k)
     vec_next(1, 2)
+    r.go_o[...] = finish(8)
     r.gq_o[...] = finish(9)
     r.gk_o[...] = finish(10)
     r.gv_o[...] = finish(11)
@@ -803,26 +884,27 @@
     two_chunks = 2 * chunks
     hd = w_query.shape[1]
     inner = [
-        ("x_raw", (total_rows, width), BF), ("x_v", (total, width), BF), ("cot_raw", (total_rows + 16, width), F32),
+        ("x_raw", (total_rows, width), BF), ("x_v", (total, width), BF),
+        ("cot_raw", (total_rows - own_rows // 8 * 8 + 16, width), F32), ("cot", (total, width), F32),
         ("bias_q", (2, 1, BLOCK), F32), ("bias_v", (2, 1, BLOCK), F32), ("bias_u", (2, 1, chunks * BLOCK), F32),
         ("b_out", (1, width), F32), ("gain_one", (1, width), F32), ("shift_one", (1, width), F32),
         ("b_down", (1, width), F32), ("gain_two", (1, width), F32), ("shift_two", (1, width), F32),
         ("wqkv", (2, 3, width, hd), BF), ("wo", (2, hd, width), BF),
         ("wu", (two_chunks, width, BLOCK), BF), ("wd", (two_chunks, BLOCK, width), BF),
         ("xT", (width + 16, items * lanes), BF), ("hT", (width + 16, items * lanes), BF),
-        ("dT", (width, items * lanes), BF),
-        ("nat", (2 * items, 3, rows_pad, hd), BF), ("tra", (2 * items, 3, hd, lanes), BF),
+        ("dT", (width, items * lanes), BF), ("oT", (width, items * lanes), BF),
+        ("keys", (2 * items, rows_pad, hd), BF), ("values", (2 * items, rows_pad, hd), BF),
+        ("tra", (2 * items, 3, hd, lanes), BF), ("score", (8, rows_pad, lanes), F32),
         ("probs", (8 * items, lanes, lanes), BF), ("ctxT", (2, hd, items * lanes), BF),
         ("ctx", (2, total, hd), BF), ("n1", (total, width), F32), ("inv1", (total, 128), F32),
         ("hlow", (total, width), BF), ("slope", (two_chunks, total, BLOCK), BF),
         ("active", (two_chunks, items, lanes, BLOCK), BF), ("acc", (total, width), F32),
-        ("out_f", (total, width), F32), ("out_v", (own_rows, width), BF), ("ig_v", (own_rows, width), F32), ("gp", (total, width), F32), ("dlow", (total, width), BF),
-        ("upg", (items, lanes, BLOCK), BF), ("olow", (items, lanes, width), BF),
-        ("cgT", (2 * items, hd, lanes), BF), ("dscore", (2, lanes, lanes), BF),
-        ("gT", (2, 3 * hd, items * lanes), BF),
-        ("g_out", (UNITS, width, BLOCK), BF), ("g_core", (UNITS, width, BLOCK), BF),
-        ("g", (UNITS, 16, shard, BLOCK), BF), ("g_a", (UNITS, 8, shard, BLOCK), BF),
-        ("g_b", (UNITS, 4, shard, BLOCK), BF), ("g_c", (UNITS, 3, shard, BLOCK), BF),
+        ("work", (3, total, BLOCK), F32), ("own", (4, width, BLOCK), F32),
+        ("out_v", (own_rows, width), BF), ("ig_v", (own_rows, width), F32), ("gp", (total, width), F32),
+        ("dlow", (total, width), BF), ("upg", (3, items, lanes, BLOCK), BF), ("olow", (items, lanes, width), BF),
+        ("cgT", (2 * items, hd, lanes), BF), ("dscore", (8, lanes, lanes), BF), ("gT", (2, 3 * hd, items * lanes), BF),
+        ("g_out", (UNITS, 16, shard, BLOCK), BF), ("g", (UNITS, 16, shard, BLOCK), BF),
+        ("g_a", (UNITS, 8, shard, BLOCK), BF), ("g_b", (UNITS, 4, shard, BLOCK), BF), ("g_c", (UNITS, 3, shard, BLOCK), BF),
         ("v_out", (2, 16, BLOCK), F32), ("v_own", (2, 16, BLOCK), F32),
         ("v_in", (2, 2 + nz, 16, BLOCK), F32), ("v_sum", (2, 3, 16, BLOCK), F32),
     ]

time: 90.5 us -> 65.5 us (0.72)
  Pallas kernels: 89.5 us -> 64.5 us
    pallas_call x1, Pallas kernels: 86.4 us -> 61.4 us  [layer_by_items(): pl.pallas_call(functools.partial(layer_kernel, (items, length, rows_pad,...]
where the time goes in v2:
time: 65.5 us; the launch traced here: 65.4 us
  Pallas kernels  64.5 us (98%)
  between operations  0.85 us (1%)
    pallas_call x1, Pallas kernels, layer_by_items(): pl.pallas_call(functools.partial(layer_kernel, (items, length, rows_pad,...  61.4 us
    pallas_call x1, Pallas kernels, layer_by_items(): pl.pallas_call(functools.partial(hand_over, count), out_shape=shapes, in_...  3.14 us

profile of v2, /device:TPU:0, one launch (start us, length us, event | category | flops | bytes accessed | tf_op | source)
XLA Modules:
  0.0 65.4 jit_solution(3943389484703068805)
XLA Ops:
  0.7 61.4 %layer.1 = (bf16[684,512]{1,0:T(8,128)(2,1)}, f32[684,512]{1,0:T(8,128)}, f32[32,256]{1,0:T(8,128)}, f32[1,256]{1,0:T(1,128)}, f32[32,256]{1,0:T(8,128)}, /*inde...) custom-call(s32[6]{0:T(128)} %refs_0_.1, ...), custom_call_target="tpu_custom_call" | custom-call | tf_op jit(solution)/shard_map/layer/pallas_call | solution.py:940
  62.1 3.1 %hand_over.1 = (bf16[684,512]{1,0:T(8,128)(2,1)}, f32[684,512]{1,0:T(8,128)}, f32[32,256]{1,0:T(8,128)}, f32[1,256]{1,0:T(1,128)}, f32[32,256]{1,0:T(8,128)}, /*...) custom-call(bf16[684,512]{1,0:T(8,128)(2,1)} %get-tuple-element.51.r, ...), custom_call_target="tpu_custom_call" | custom-call | tf_op jit(solution)/shard_map/hand_over/pallas_call | solution.py:951

commit v3 on v2

--- a/solution.py
+++ b/solution.py
@@ -250,7 +250,7 @@
 BLOCK = 256
 UNITS = 12
 X_FIRST, Y_FIRST, Z_FIRST = 0, 1, 2
-ORDER = (0, 1, 2, 0, 1, 2, 0, 1, 1, 1, 2, 0)
+ORDER = (2, 0, 1, 2, 0, 1, 0, 1, 0, 1, 0, 1)
 
 
 def dot_nn(a, b):
@@ -292,6 +292,11 @@
     c_x = bring(r.x_h, r.x_raw)
     c_w = [bring(src, r.wqkv.at[0, k]) for k, src in enumerate((r.wq_h, r.wk_h, r.wv_h))]
     c_p = [bring(r.b_query_h, r.bias_q.at[0]), bring(r.b_value_h, r.bias_v.at[0]), bring(r.b_up_h, r.bias_u.at[0])]
+
+    barrier = pltpu.get_barrier_semaphore()
+    near = [core] + plane_side + z_side
+    for device in near:
+        pl.semaphore_signal(barrier, inc=1, device_id=device, device_id_type=MESH)
     vectors = (
         (r.b_out_h, r.b_out), (r.gain_one_h, r.gain_one), (r.shift_one_h, r.shift_one),
         (r.b_down_h, r.b_down), (r.gain_two_h, r.gain_two), (r.shift_two_h, r.shift_two))
@@ -304,30 +309,6 @@
     cot_count = full_rows - base
     c_cot = bring(r.cot_h.at[pl.ds(pl.multiple_of(mp * base, 8), cot_count)], r.cot_raw.at[pl.ds(0, cot_count)])
 
-    barrier = pltpu.get_barrier_semaphore()
-    near = [core] + plane_side + z_side
-    for device in near:
-        pl.semaphore_signal(barrier, inc=1, device_id=device, device_id_type=MESH)
-    pl.semaphore_wait(barrier, len(near))
-
-    remote = []
-
-    def send_weight(src, dst):
-        k = len(remote)
-        copy = pltpu.make_async_remote_copy(
-            src_ref=src, dst_ref=dst, send_sem=r.w_send.at[k], recv_sem=r.w_recv.at[k],
-            device_id=core, device_id_type=MESH)
-        copy.start()
-        remote.append(copy)
-        return copy
-
-    s_w = [send_weight(src, r.wqkv.at[1, k]) for k, src in enumerate((r.wq_h, r.wk_h, r.wv_h))]
-    s_w += [send_weight(src, dst.at[1]) for src, dst in (
-        (r.b_query_h, r.bias_q), (r.b_value_h, r.bias_v), (r.b_up_h, r.bias_u))]
-    s_wo = send_weight(r.wo_h, r.wo.at[1])
-    s_wu = [send_weight(r.wu_h.at[:, pl.ds(c * BLOCK, BLOCK)], r.wu.at[chunks + c]) for c in range(chunks)]
-    s_wd = send_weight(r.wd_h, r.wd.at[pl.ds(chunks, chunks)])
-
     pad_rows = lanes - rows_pad
 
     def transposed(block):
@@ -339,6 +320,9 @@
 
     def lanes_of(i):
         return pl.ds(pl.multiple_of(i * lanes, lanes), lanes)
+
+    def greet():
+        pl.semaphore_wait(barrier, len(near))
 
     def clear(n, carry):
         r.probs[n, pl.ds(rows_pad, pad_rows), :] = jnp.zeros((pad_rows, lanes), BF)
@@ -374,6 +358,26 @@
             term = dot_nn(pick[:, :count], r.x_raw[pl.ds(window, count), :])
             block = term if block is None else block + term
         r.x_v[rows_of(i), :] = block.astype(BF)
+
+    greet()
+
+    remote = []
+
+    def send_weight(src, dst):
+        k = len(remote)
+        copy = pltpu.make_async_remote_copy(
+            src_ref=src, dst_ref=dst, send_sem=r.w_send.at[k], recv_sem=r.w_recv.at[k],
+            device_id=core, device_id_type=MESH)
+        copy.start()
+        remote.append(copy)
+        return copy
+
+    s_w = [send_weight(src, r.wqkv.at[1, k]) for k, src in enumerate((r.wq_h, r.wk_h, r.wv_h))]
+    s_w += [send_weight(src, dst.at[1]) for src, dst in (
+        (r.b_query_h, r.bias_q), (r.b_value_h, r.bias_v), (r.b_up_h, r.bias_u))]
+    s_wo = send_weight(r.wo_h, r.wo.at[1])
+    s_wu = [send_weight(r.wu_h.at[:, pl.ds(c * BLOCK, BLOCK)], r.wu.at[chunks + c]) for c in range(chunks)]
+    s_wd = send_weight(r.wd_h, r.wd.at[pl.ds(chunks, chunks)])
 
     def project(slot, k):
         r.work[k] = dot_nn(r.x_v[...], r.wqkv[slot, k])
@@ -591,14 +595,14 @@
 
     def start_b(u):
         order = ORDER[u]
-        stage_a(u, order).wait()
+        stage_a(u, order).wait_recv()
         kept = pl.ds(route[order][0] * 8, 8)
         r.g[u, kept] = r.g[u, kept] + r.g_a[u]
         stage_b(u, order).start()
 
     def start_c(u):
         order = ORDER[u]
-        stage_b(u, order).wait()
+        stage_b(u, order).wait_recv()
         kept = pl.ds(route[order][0] * 8 + route[order][1] * 4, 4)
         r.g[u, kept] = r.g[u, kept] + r.g_b[u]
         for step in range(1, 4):
@@ -609,7 +613,7 @@
         first, second, third, _, _ = route[order]
         acc = r.g[u, first * 8 + second * 4 + third].astype(F32)
         for step in range(1, 4):
-            stage_c(u, order, step).wait()
+            stage_c(u, order, step).wait_recv()
             acc += r.g_c[u, step - 1].astype(F32)
         return acc
 
@@ -629,21 +633,21 @@
 
     def vec_next(k, stage):
         if stage == 0:
-            vec_core(k).wait()
+            vec_core(k).wait_recv()
             r.v_sum[k, 0] = r.v_own[k] + r.v_in[k, 0]
             vec_side(k, 1).start()
         elif stage == 1:
-            vec_side(k, 1).wait()
+            vec_side(k, 1).wait_recv()
             r.v_sum[k, 1] = r.v_sum[k, 0] + r.v_in[k, 1]
             vec_side(k, 2).start()
         elif stage == 2:
-            vec_side(k, 2).wait()
+            vec_side(k, 2).wait_recv()
             r.v_sum[k, 2] = r.v_sum[k, 1] + r.v_in[k, 2]
             for step in range(1, nz):
                 vec_z(k, step).start()
         else:
             for step in range(1, nz):
-                vec_z(k, step).wait()
+                vec_z(k, step).wait_recv()
             terms = [r.v_sum[k, 2]] + [r.v_in[k, 2 + step] for step in range(1, nz)]
             acc = jnp.zeros(terms[0].shape, F32)
             for zz in range(nz):
@@ -696,9 +700,7 @@
         hold(c, down_grad(c))
         if c < items:
             turn(c)
-    r.out_v[...] = r.acc[pl.ds(0, items * length), :].astype(BF)
-    out_copy = pltpu.make_async_copy(r.out_v, r.out_h, r.out_sem.at[0])
-    out_copy.start()
+    r.out_o[...] = r.acc[pl.ds(0, items * length), :].astype(BF)
     order = list(range(chunks, 2 * chunks)) + list(range(chunks))
     active_grad(order[0])
     for c in range(chunks):
@@ -819,9 +821,7 @@
             for k in range(3):
                 term = dot_nn(r.wqkv[slot, k], r.gT[slot, pl.ds(k * 256, 256), pl.ds(i * lanes, lanes)])
                 acc = term if acc is None else acc + term
-        r.ig_v[pl.ds(i * length, length), :] = acc.T[:length] + r.gp[pl.ds(i * rows_pad, length), :]
-    grad_copy = pltpu.make_async_copy(r.ig_v, r.ig_h, r.out_sem.at[1])
-    grad_copy.start()
+        r.ig_o[pl.ds(i * length, length), :] = acc.T[:length] + r.gp[pl.ds(i * rows_pad, length), :]
     start_b(8)
     start_c(5)
     start_c(6)
@@ -847,21 +847,25 @@
         s.wait_send()
     for u in range(UNITS):
         to_core(u).wait_send()
-    out_copy.wait()
-    grad_copy.wait()
+        stage_a(u, ORDER[u]).wait_send()
+        stage_b(u, ORDER[u]).wait_send()
+        for step in range(1, 4):
+            stage_c(u, ORDER[u], step).wait_send()
+    for k in range(2):
+        vec_core(k).wait_send()
+        vec_side(k, 1).wait_send()
+        vec_side(k, 2).wait_send()
+        for step in range(1, nz):
+            vec_z(k, step).wait_send()
 
 
 def hand_over(count, *refs):
-    held, sems = refs[2 * count:3 * count], refs[-1]
-    into = [pltpu.make_async_copy(refs[k], held[k], sems.at[0, k]) for k in range(count)]
-    out = [pltpu.make_async_copy(held[k], refs[count + k], sems.at[1, k]) for k in range(count)]
-    for c in into:
+    sems = refs[-1]
+    copies = [pltpu.make_async_copy(refs[k], refs[count + k], sems.at[k]) for k in range(count)]
+    for c in copies:
         c.start()
-    for c, d in zip(into, out, strict=True):
+    for c in copies:
         c.wait()
-        d.start()
-    for d in out:
-        d.wait()
 
 
 def layer_by_items(
@@ -900,7 +904,7 @@
         ("hlow", (total, width), BF), ("slope", (two_chunks, total, BLOCK), BF),
         ("active", (two_chunks, items, lanes, BLOCK), BF), ("acc", (total, width), F32),
         ("work", (3, total, BLOCK), F32), ("own", (4, width, BLOCK), F32),
-        ("out_v", (own_rows, width), BF), ("ig_v", (own_rows, width), F32), ("gp", (total, width), F32),
+        ("gp", (total, width), F32),
         ("dlow", (total, width), BF), ("upg", (3, items, lanes, BLOCK), BF), ("olow", (items, lanes, width), BF),
         ("cgT", (2 * items, hd, lanes), BF), ("dscore", (8, lanes, lanes), BF), ("gT", (2, 3 * hd, items * lanes), BF),
         ("g_out", (UNITS, 16, shard, BLOCK), BF), ("g", (UNITS, 16, shard, BLOCK), BF),
@@ -910,7 +914,7 @@
     ]
     n_weights = 8 + chunks
     sems = [
-        ("in_sem", (16 + chunks,)), ("w_send", (n_weights,)), ("w_recv", (n_weights,)), ("out_sem", (2,)),
+        ("in_sem", (16 + chunks,)), ("w_send", (n_weights,)), ("w_recv", (n_weights,)),
         ("core_send", (UNITS,)), ("core_recv", (UNITS,)), ("a_send", (UNITS,)), ("a_recv", (UNITS,)),
         ("b_send", (UNITS,)), ("b_recv", (UNITS,)), ("c_send", (UNITS, 3)), ("c_recv", (UNITS, 3)),
         ("v_send", (2, 2 + nz)), ("v_recv", (2, 2 + nz)),
@@ -924,38 +928,39 @@
     ]
     hidden = chunks * BLOCK
     results = [
-        ("out_h", (own_rows, width), BF, pl.ANY), ("ig_h", (own_rows, width), F32, pl.ANY),
-        ("gq_o", (shard, hd), F32, pltpu.VMEM), ("bq_o", (1, hd), F32, pltpu.VMEM),
-        ("gk_o", (shard, hd), F32, pltpu.VMEM), ("gv_o", (shard, hd), F32, pltpu.VMEM),
-        ("bv_o", (1, hd), F32, pltpu.VMEM), ("go_o", (shard, hd), F32, pltpu.VMEM),
-        ("bout_o", (1, width), F32, pltpu.VMEM), ("gain1_o", (1, width), F32, pltpu.VMEM),
-        ("shift1_o", (1, width), F32, pltpu.VMEM), ("gu_o", (shard, hidden), F32, pltpu.VMEM),
-        ("bup_o", (1, hidden), F32, pltpu.VMEM), ("gd_o", (shard, hidden), F32, pltpu.VMEM),
-        ("bdown_o", (1, width), F32, pltpu.VMEM), ("gain2_o", (1, width), F32, pltpu.VMEM),
-        ("shift2_o", (1, width), F32, pltpu.VMEM),
+        ("out_o", (own_rows, width), BF), ("ig_o", (own_rows, width), F32),
+        ("gq_o", (shard, hd), F32), ("bq_o", (1, hd), F32),
+        ("gk_o", (shard, hd), F32), ("gv_o", (shard, hd), F32),
+        ("bv_o", (1, hd), F32), ("go_o", (shard, hd), F32),
+        ("bout_o", (1, width), F32), ("gain1_o", (1, width), F32),
+        ("shift1_o", (1, width), F32), ("gu_o", (shard, hidden), F32),
+        ("bup_o", (1, hidden), F32), ("gd_o", (shard, hidden), F32),
+        ("bdown_o", (1, width), F32), ("gain2_o", (1, width), F32),
+        ("shift2_o", (1, width), F32),
     ]
     names = [n for n, _ in operands] + [n for n, *_ in results] + [n for n, *_ in inner] + [n for n, _ in sems]
     smem = pl.BlockSpec(memory_space=pltpu.SMEM)
-    shapes = [jax.ShapeDtypeStruct(s, d) for _, s, d, _ in results]
+    shapes = [jax.ShapeDtypeStruct(s, d) for _, s, d in results]
     made = pl.pallas_call(
         functools.partial(layer_kernel, (items, length, rows_pad, lanes, nz, shard), names),
-        out_shape=shapes,
+        out_shape=[pltpu.VMEM(s, d) for _, s, d in results],
         in_specs=[smem] + [pl.BlockSpec(memory_space=pl.ANY)] * (len(operands) - 1),
-        out_specs=[pl.BlockSpec(memory_space=m) for *_, m in results],
+        out_specs=[pl.BlockSpec(memory_space=pltpu.VMEM)] * len(results),
         scratch_shapes=[pltpu.VMEM(s, d) for _, s, d in inner] + [pltpu.SemaphoreType.DMA(s) for _, s in sems],
         compiler_params=pltpu.CompilerParams(
-            collective_id=0, has_side_effects=True, vmem_limit_bytes=63 * 2**20),
+            collective_id=0, has_side_effects=True, vmem_limit_bytes=59 * 2**20),
         name="layer",
     )(*[v for _, v in operands])
     count = len(shapes)
     made = pl.pallas_call(
         functools.partial(hand_over, count),
         out_shape=shapes,
-        in_specs=[pl.BlockSpec(memory_space=pl.ANY)] * count,
+        in_specs=[pl.BlockSpec(memory_space=pltpu.VMEM)] * count,
         out_specs=[pl.BlockSpec(memory_space=pl.ANY)] * count,
-        scratch_shapes=[pltpu.VMEM(s.shape, s.dtype) for s in shapes] + [pltpu.SemaphoreType.DMA((2, count))],
+        scratch_shapes=[pltpu.SemaphoreType.DMA((count,))],
+        compiler_params=pltpu.CompilerParams(vmem_limit_bytes=2**20),
         name="hand_over",
-    )(*made)
+    )(*[pltpu.with_memory_space_constraint(v, pltpu.VMEM) for v in made])
     made = [v.reshape(-1) if v.shape[0] == 1 else v for v in made]
     made[7], made[13] = made[7].T, made[13].T
     return tuple(made)

time: 65.5 us -> 63.3 us (0.966)
  Pallas kernels: 64.5 us -> 62.3 us
    pallas_call x1, Pallas kernels: 3.14 us -> 1.64 us  [layer_by_items(): pl.pallas_call(functools.partial(hand_over, count), out_shape=shapes, in_...]
    pallas_call x1, Pallas kernels: 61.4 us -> 60.7 us  [layer_by_items(): pl.pallas_call(functools.partial(layer_kernel, (items, length, rows_pad,...]
where the time goes in v3:
time: 63.3 us; the launch traced here: 63.2 us
  Pallas kernels  62.3 us (98%)
  between operations  0.85 us (1%)
    pallas_call x1, Pallas kernels, layer_by_items(): pl.pallas_call(functools.partial(layer_kernel, (items, length, rows_pad,...  60.7 us
    pallas_call x1, Pallas kernels, layer_by_items(): pl.pallas_call(functools.partial(hand_over, count), out_shape=shapes, in_...  1.64 us

profile of v3, /device:TPU:0, one launch (start us, length us, event | category | flops | bytes accessed | tf_op | source)
XLA Modules:
  0.0 63.2 jit_solution(144252092940125542)
XLA Ops:
  0.7 60.7 %layer.1 = (bf16[684,512]{1,0:T(8,128)(2,1)S(1)}, f32[684,512]{1,0:T(8,128)S(1)}, f32[32,256]{1,0:T(8,128)S(1)}, f32[1,256]{1,0:T(1,128)S(1)}, f32[32,256]{1,0:T...) custom-call(s32[6]{0:T(128)} %refs_0_.1, ...), custom_call_target="tpu_custom_call" | custom-call | tf_op jit(solution)/shard_map/layer/pallas_call | solution.py:944
  61.4 1.6 %hand_over.1 = (bf16[684,512]{1,0:T(8,128)(2,1)}, f32[684,512]{1,0:T(8,128)}, f32[32,256]{1,0:T(8,128)}, f32[1,256]{1,0:T(1,128)}, f32[32,256]{1,0:T(8,128)}, /*...) custom-call(bf16[684,512]{1,0:T(8,128)(2,1)S(1)} %get-tuple-element., ...), custom_call_target="tpu_custom_call" | custom-call | tf_op jit(solution)/shard_map/hand_over/pallas_call | solution.py:955

commit v4 on v3

--- a/solution.py
+++ b/solution.py
@@ -248,9 +248,32 @@
 BF = jnp.bfloat16
 F32 = jnp.float32
 BLOCK = 256
-UNITS = 12
+HALF = 128
+WHOLE_UNITS, HALF_UNITS = 9, 6
+UNITS = WHOLE_UNITS + HALF_UNITS
 X_FIRST, Y_FIRST, Z_FIRST = 0, 1, 2
-ORDER = (2, 0, 1, 2, 0, 1, 0, 1, 0, 1, 0, 1)
+ORDER = (0, 1, 2, 0, 1, 2, 1, 1, 2, 0, 1, 0, 1, 0, 1)
+PLAN = {
+    13: (('M', 0, 1, 2, 3),),
+    14: (('A', 0, 1),),
+    21: (('M', 4, 5),),
+    23: (('M', 6, 7),),
+    24: (('A', 4),),
+    25: (('A', 5),),
+    26: (('B', 0, 1), ('A', 6),),
+    27: (('B', 2), ('A', 7),),
+    31: (('M', 8), ('D', -1), ('C', 1), ('B', 3, 4),),
+    41: (('D', 0), ('A', 8), ('C', 0), ('B', 5),),
+    43: (('M', 9, 10, 11, 12, 13, 14), ('E', -1), ('C', 2),),
+    51: (('C', 4), ('B', 6),),
+    53: (('D', 1), ('A', 9, 10, 11),),
+    61: (('B', 7),),
+    63: (('D', 2), ('E', 0), ('A', 12, 13, 14), ('C', 3), ('B', 8),),
+    71: (('C', 5, 6), ('B', 9, 10, 11),),
+    72: (('C', 7),),
+    73: (('E', 1), ('B', 12, 13, 14), ('F', 0, 1, 2), ('C', 9, 10, 11), ('D', 3), ('E', 2), ('F', 3, 4), ('C', 12, 13, 14), ('C', 8), ('F', 5, 6, 7), ('F', 8, 9, 10, 11, 12, 13, 14), ('E', 3), ('D', 4), ('E', 4),),
+    20: (('A', 2, 3),),
+}
 
 
 def dot_nn(a, b):
@@ -401,11 +424,6 @@
         project(0, k)
     for k in range(3):
         keep(0, k)
-    for c in s_w:
-        c.wait_recv()
-    for k in range(3):
-        project(1, k)
-
     lane = lax.broadcasted_iota(jnp.int32, (1, 128), 1)
     half = [jnp.where(lane < 64, 1.0, 0.0).astype(BF), jnp.where(lane >= 64, 1.0, 0.0).astype(BF)]
     position = lax.broadcasted_iota(jnp.int32, (rows_pad, lanes), 0)
@@ -438,10 +456,18 @@
 
     scores_of(0)
     for n in range(2 * items):
+        if n + 1 == items:
+            soften(n)
+            for c in s_w:
+                c.wait_recv()
+            for k in range(3):
+                project(1, k)
+            contexts_of(n)
+            for k in range(3):
+                keep(1, k)
+            scores_of(n + 1)
+            continue
         if n + 1 < 2 * items:
-            if n + 1 == items:
-                for k in range(3):
-                    keep(1, k)
             scores_of(n + 1)
         soften(n)
         contexts_of(n)
@@ -540,9 +566,17 @@
     for i in range(items):
         second_norm(i)
 
+    def held(u):
+        if u < WHOLE_UNITS:
+            return [ref.at[u] for ref in (r.g_out, r.g, r.g_a, r.g_b, r.g_c)]
+        return [ref.at[u - WHOLE_UNITS] for ref in (r.h_out, r.h, r.h_a, r.h_b, r.h_c)]
+
+    def size_of(u):
+        return 0 if u < WHOLE_UNITS else 1
+
     def to_core(u):
         return pltpu.make_async_remote_copy(
-            src_ref=r.g_out.at[u], dst_ref=r.g.at[u], send_sem=r.core_send.at[u],
+            src_ref=held(u)[0], dst_ref=held(u)[1], send_sem=r.sent.at[0, size_of(u)],
             recv_sem=r.core_recv.at[u], device_id=core, device_id_type=MESH)
 
     route = (
@@ -558,14 +592,27 @@
     def stage_a(u, order):
         first, _, _, device, _ = route[order]
         return pltpu.make_async_remote_copy(
-            src_ref=r.g.at[u, pl.ds((1 - first) * 8, 8)], dst_ref=r.g_a.at[u], send_sem=r.a_send.at[u],
+            src_ref=held(u)[1].at[pl.ds((1 - first) * 8, 8)], dst_ref=held(u)[2], send_sem=r.sent.at[1, size_of(u)],
             recv_sem=r.a_recv.at[u], device_id=device, device_id_type=MESH)
 
     def stage_b(u, order):
         first, second, _, _, device = route[order]
         return pltpu.make_async_remote_copy(
-            src_ref=r.g.at[u, pl.ds(first * 8 + (1 - second) * 4, 4)], dst_ref=r.g_b.at[u], send_sem=r.b_send.at[u],
+            src_ref=held(u)[1].at[pl.ds(first * 8 + (1 - second) * 4, 4)], dst_ref=held(u)[3], send_sem=r.sent.at[2, size_of(u)],
             recv_sem=r.b_recv.at[u], device_id=device, device_id_type=MESH)
+
+    def wait_spread(u):
+        came = held(u)[4]
+        pltpu.make_async_remote_copy(
+            src_ref=came, dst_ref=came, send_sem=r.sent.at[3, size_of(u)], recv_sem=r.c_recv.at[u],
+            device_id=core, device_id_type=MESH).wait_recv()
+
+    def wait_sent():
+        for size, bufs in enumerate(((r.g_out, r.g_a, r.g_b, r.g_c), (r.h_out, r.h_a, r.h_b, r.h_c))):
+            for stage, ref in enumerate(bufs):
+                pltpu.make_async_remote_copy(
+                    src_ref=ref, dst_ref=ref, send_sem=r.sent.at[stage, size], recv_sem=r.core_recv.at[0],
+                    device_id=core, device_id_type=MESH).wait_send()
 
     def stage_c(u, order, step):
         first, second, _, _, _ = route[order]
@@ -574,53 +621,67 @@
         else:
             place, device = ((y + step // 2) % 2) * 2 + (x + step) % 2, plane_side[step - 1]
         return pltpu.make_async_remote_copy(
-            src_ref=r.g.at[u, first * 8 + second * 4 + place], dst_ref=r.g_c.at[u, step - 1],
-            send_sem=r.c_send.at[u, step - 1], recv_sem=r.c_recv.at[u, step - 1],
+            src_ref=held(u)[1].at[first * 8 + second * 4 + place], dst_ref=held(u)[4].at[step - 1],
+            send_sem=r.sent.at[3, size_of(u)], recv_sem=r.c_recv.at[u],
             device_id=device, device_id_type=MESH)
 
-    def start_core(u, value):
+    def lay_out(u, value):
+        ref = held(u)[0]
         for place, block in enumerate(shard_order(ORDER[u])):
-            r.g_out[u, place] = value[block * shard:(block + 1) * shard].astype(BF)
+            ref[place] = value[block * shard:(block + 1) * shard].astype(BF)
+
+    def start_core(u):
         to_core(u).start()
 
     def hold(u, value):
-        r.own[u % r.own.shape[0]] = value
+        r.own[u % r.own.shape[0], :, :value.shape[1]] = value
 
     def start_a(u):
         to_core(u).wait_recv()
+        ref = held(u)[1]
         for place, block in enumerate(shard_order(ORDER[u])):
-            mine = r.own[u % r.own.shape[0], pl.ds(block * shard, shard), :]
-            r.g[u, place] = (mine + r.g[u, place].astype(F32)).astype(BF)
+            mine = r.own[u % r.own.shape[0], pl.ds(block * shard, shard), :ref.shape[-1]]
+            ref[place] = (mine + ref[place].astype(F32)).astype(BF)
         stage_a(u, ORDER[u]).start()
 
     def start_b(u):
         order = ORDER[u]
         stage_a(u, order).wait_recv()
         kept = pl.ds(route[order][0] * 8, 8)
-        r.g[u, kept] = r.g[u, kept] + r.g_a[u]
+        _, ref, came, _, _ = held(u)
+        ref[kept] = ref[kept] + came[...]
         stage_b(u, order).start()
 
     def start_c(u):
         order = ORDER[u]
         stage_b(u, order).wait_recv()
         kept = pl.ds(route[order][0] * 8 + route[order][1] * 4, 4)
-        r.g[u, kept] = r.g[u, kept] + r.g_b[u]
+        _, ref, _, came, _ = held(u)
+        ref[kept] = ref[kept] + came[...]
         for step in range(1, 4):
             stage_c(u, order, step).start()
 
     def finish(u):
         order = ORDER[u]
         first, second, third, _, _ = route[order]
-        acc = r.g[u, first * 8 + second * 4 + third].astype(F32)
+        _, ref, _, _, came = held(u)
+        acc = ref[first * 8 + second * 4 + third].astype(F32)
+        wait_spread(u)
         for step in range(1, 4):
-            stage_c(u, order, step).wait_recv()
-            acc += r.g_c[u, step - 1].astype(F32)
+            acc += came[step - 1].astype(F32)
         return acc
 
     def vec_copy(k, stage, src, device):
+        group = min(stage, 3)
         return pltpu.make_async_remote_copy(
-            src_ref=src, dst_ref=r.v_in.at[k, stage], send_sem=r.v_send.at[k, stage],
-            recv_sem=r.v_recv.at[k, stage], device_id=device, device_id_type=MESH)
+            src_ref=src, dst_ref=r.v_in.at[k, stage], send_sem=r.v_send.at[k, group],
+            recv_sem=r.v_recv.at[k, group], device_id=device, device_id_type=MESH)
+
+    def vec_spread(k):
+        came = r.v_in.at[k, pl.ds(3, nz - 1)]
+        return pltpu.make_async_remote_copy(
+            src_ref=came, dst_ref=came, send_sem=r.v_send.at[k, 3], recv_sem=r.v_recv.at[k, 3],
+            device_id=core, device_id_type=MESH)
 
     def vec_core(k):
         return vec_copy(k, 0, r.v_out.at[k], core)
@@ -646,8 +707,7 @@
             for step in range(1, nz):
                 vec_z(k, step).start()
         else:
-            for step in range(1, nz):
-                vec_z(k, step).wait_recv()
+            vec_spread(k).wait_recv()
             terms = [r.v_sum[k, 2]] + [r.v_in[k, 2 + step] for step in range(1, nz)]
             acc = jnp.zeros(terms[0].shape, F32)
             for zz in range(nz):
@@ -666,6 +726,38 @@
                 r.bq_o[...] = acc[0:1]
                 r.bv_o[...] = acc[1:2]
 
+    def store_sum(u):
+        total_ = finish(u)
+        if u < 2 * chunks:
+            column = u % chunks * BLOCK
+            (r.gd_o, r.gu_o)[u // chunks][:, column:column + BLOCK] = total_
+        elif u < WHOLE_UNITS:
+            r.go_o[...] = total_
+        else:
+            column = (u - WHOLE_UNITS) // 3 * HALF
+            (r.gq_o, r.gk_o, r.gv_o)[(u - WHOLE_UNITS) % 3][:, column:column + HALF] = total_
+
+    def sums(k):
+        def step(stage):
+            if stage == 4:
+                vec_core(k).wait_send()
+                vec_side(k, 1).wait_send()
+                vec_side(k, 2).wait_send()
+                vec_spread(k).wait_send()
+            elif stage < 0:
+                vec_core(k).start()
+            else:
+                vec_next(k, stage)
+
+        return step
+
+    steps = dict(M=start_core, A=start_a, B=start_b, C=start_c, F=store_sum, D=sums(0), E=sums(1))
+
+    def after(piece):
+        for step, *units in PLAN.get(piece, ()):
+            for u in units:
+                steps[step](u)
+
     def down_grad(j):
         return dot_nn(r.dT[...], r.active[j].reshape(items * lanes, BLOCK))
 
@@ -695,7 +787,8 @@
         r.tra[n, 1] = transposed(r.keys[n].astype(F32) * 0.125)
 
     for c in range(chunks):
-        start_core(c, down_grad(chunks + c))
+        lay_out(c, down_grad(chunks + c))
+        after(10 + c)
     for c in range(chunks):
         hold(c, down_grad(c))
         if c < items:
@@ -703,8 +796,7 @@
     r.out_o[...] = r.acc[pl.ds(0, items * length), :].astype(BF)
     order = list(range(chunks, 2 * chunks)) + list(range(chunks))
     active_grad(order[0])
-    for c in range(chunks):
-        start_a(c)
+    after(14)
     for k, j in enumerate(order):
         if k + 1 < 2 * chunks:
             active_grad(order[k + 1])
@@ -712,7 +804,7 @@
         up = up_grad(j)
         c = j % chunks
         if j >= chunks:
-            start_core(chunks + c, up)
+            lay_out(chunks + c, up)
             r.v_out[0, pl.ds(12 + c, 1), :] = up[width:width + 1]
         else:
             hold(chunks + c, up[:width])
@@ -722,11 +814,8 @@
             turn_keys(k)
         else:
             turn_input(k - 2 * items)
-        if j < chunks:
-            start_a(chunks + c)
+        after(20 + k)
     turn_input(2)
-    for u in range(3):
-        start_b(u)
 
     bout, gain1, shift1 = [], [], []
 
@@ -752,33 +841,34 @@
             piece = v[:, part * BLOCK:(part + 1) * BLOCK]
             r.v_out[0, pl.ds(2 * k + part, 1), :] = piece
             r.v_own[0, pl.ds(2 * k + part, 1), :] = piece
-    vec_core(0).start()
-
-    start_core(8, dot_nt(r.oT[...], r.ctxT[1]))
+    after(30)
+
+    lay_out(8, dot_nt(r.oT[...], r.ctxT[1]))
     for n in [*range(items, 2 * items), *range(items)]:
         r.cgT[n] = dot_nt(r.wo[n // items], r.olow[n % items]).astype(BF)
     hold(8, dot_nt(r.oT[...], r.ctxT[0]))
-
-    def probs_grad(n):
-        for h in range(4):
+    after(31)
+
+    def probs_grad(n, heads):
+        for h in heads:
             r.score[(n % 2) * 4 + h] = dot_nn(r.values[n, :, pair_of(h)] * half[h % 2], r.cgT[n, pair_of(h), :])
 
     def store_grad(n, k, h, value):
         r.gT[n // items, pl.ds(k * 256 + h * 64, 64), pl.ds((n % items) * lanes, lanes)] = value.astype(BF)
 
-    def value_grad(n):
-        for h in range(4):
+    def value_grad(n, heads):
+        for h in heads:
             store_grad(n, 2, h, dot_nt(r.cgT[n, head_of(h), :], r.probs[n * 4 + h]))
 
-    def score_grad(n):
-        for h in range(4):
+    def score_grad(n, heads):
+        for h in heads:
             pg = r.score[(n % 2) * 4 + h]
             p = r.probs[n * 4 + h, pl.ds(0, rows_pad), :].astype(F32)
             inner = jnp.sum(p * pg, axis=0, keepdims=True)
             r.dscore[(n % 2) * 4 + h, pl.ds(0, rows_pad), :] = (p * (pg - inner)).astype(BF)
 
-    def query_key_grad(n):
-        for h in range(4):
+    def query_key_grad(n, heads):
+        for h in heads:
             ds = r.dscore[(n % 2) * 4 + h]
             store_grad(n, 0, h, dot_nn(r.tra[n, 1, head_of(h), :], ds))
             store_grad(n, 1, h, dot_nt(r.tra[n, 0, head_of(h), :], ds))
@@ -786,77 +876,49 @@
     def projection_grad(slot, k):
         return dot_nt(r.xT[...], r.gT[slot, pl.ds(k * 256, 256), :])
 
-    after = (
-        lambda: (start_a(8), vec_next(0, 0)),
-        lambda: start_b(3),
-        lambda: (start_c(0), start_c(1), start_c(2), vec_next(0, 1)),
-        lambda: (start_b(4), start_b(5)),
-        lambda: (start_b(6), start_c(3)),
-        lambda: (start_b(7), start_c(4), vec_next(0, 2)))
-    for k in range(2 * items):
-        n = (k + items) % (2 * items)
-        probs_grad(n)
-        value_grad(n)
-        score_grad(n)
-        query_key_grad(n)
-        if k == items - 1:
-            for part in range(3):
-                grad = projection_grad(1, part)
-                start_core(9 + part, grad)
-                if part != 1:
-                    r.v_out[1, pl.ds(part // 2, 1), :] = grad[width:width + 1]
-            vec_core(1).start()
-        after[k]()
+    for s in remote:
+        s.wait_send()
+
+    def attend_back(n, heads):
+        probs_grad(n, heads)
+        value_grad(n, heads)
+        score_grad(n, heads)
+        query_key_grad(n, heads)
+
+    for n in range(items, 2 * items):
+        attend_back(n, range(4))
+        after(40 + n - items)
     for part in range(3):
-        grad = projection_grad(0, part)
-        hold(9 + part, grad[:width])
+        grad = projection_grad(1, part)
+        for pair in range(2):
+            lay_out(WHOLE_UNITS + 3 * pair + part, grad[:, pair * HALF:(pair + 1) * HALF])
         if part != 1:
-            r.v_own[1, pl.ds(part // 2, 1), :] = grad[width:width + 1]
-        start_a(9 + part)
-    vec_next(1, 0)
+            r.v_out[1, pl.ds(part // 2, 1), :] = grad[width:width + 1]
+    after(43)
+    for pair in range(2):
+        for n in range(items):
+            attend_back(n, (2 * pair, 2 * pair + 1))
+            after(50 + 10 * pair + n)
+        rows = [r.gT[0, pl.ds(part * BLOCK + pair * HALF, HALF), :] for part in range(3)]
+        grad = dot_nt(r.xT[...], jnp.concatenate(rows, axis=0))
+        for part in range(3):
+            columns = slice(part * HALF, (part + 1) * HALF)
+            hold(WHOLE_UNITS + 3 * pair + part, grad[:width, columns])
+            if part != 1:
+                r.v_own[1, pl.ds(part // 2, 1), pair * HALF:(pair + 1) * HALF] = grad[width:width + 1, columns]
+        after(53 + 10 * pair)
 
     for i in range(items):
+        if i > 0:
+            after(70 + i)
         acc = None
         for slot in range(2):
             for k in range(3):
                 term = dot_nn(r.wqkv[slot, k], r.gT[slot, pl.ds(k * 256, 256), pl.ds(i * lanes, lanes)])
                 acc = term if acc is None else acc + term
         r.ig_o[pl.ds(i * length, length), :] = acc.T[:length] + r.gp[pl.ds(i * rows_pad, length), :]
-    start_b(8)
-    start_c(5)
-    start_c(6)
-    start_c(7)
-    for k in range(3):
-        start_b(9 + k)
-    vec_next(1, 1)
-    start_c(8)
-    vec_next(0, 3)
-    for c in range(chunks):
-        r.gd_o[:, c * BLOCK:(c + 1) * BLOCK] = finish(c)
-        r.gu_o[:, c * BLOCK:(c + 1) * BLOCK] = finish(chunks + c)
-    for k in range(3):
-        start_c(9 + k)
-    vec_next(1, 2)
-    r.go_o[...] = finish(8)
-    r.gq_o[...] = finish(9)
-    r.gk_o[...] = finish(10)
-    r.gv_o[...] = finish(11)
-    vec_next(1, 3)
-
-    for s in remote:
-        s.wait_send()
-    for u in range(UNITS):
-        to_core(u).wait_send()
-        stage_a(u, ORDER[u]).wait_send()
-        stage_b(u, ORDER[u]).wait_send()
-        for step in range(1, 4):
-            stage_c(u, ORDER[u], step).wait_send()
-    for k in range(2):
-        vec_core(k).wait_send()
-        vec_side(k, 1).wait_send()
-        vec_side(k, 2).wait_send()
-        for step in range(1, nz):
-            vec_z(k, step).wait_send()
+    after(73)
+    wait_sent()
 
 
 def hand_over(count, *refs):
@@ -907,17 +969,20 @@
         ("gp", (total, width), F32),
         ("dlow", (total, width), BF), ("upg", (3, items, lanes, BLOCK), BF), ("olow", (items, lanes, width), BF),
         ("cgT", (2 * items, hd, lanes), BF), ("dscore", (8, lanes, lanes), BF), ("gT", (2, 3 * hd, items * lanes), BF),
-        ("g_out", (UNITS, 16, shard, BLOCK), BF), ("g", (UNITS, 16, shard, BLOCK), BF),
-        ("g_a", (UNITS, 8, shard, BLOCK), BF), ("g_b", (UNITS, 4, shard, BLOCK), BF), ("g_c", (UNITS, 3, shard, BLOCK), BF),
+        ("g_out", (WHOLE_UNITS, 16, shard, BLOCK), BF), ("g", (WHOLE_UNITS, 16, shard, BLOCK), BF),
+        ("g_a", (WHOLE_UNITS, 8, shard, BLOCK), BF), ("g_b", (WHOLE_UNITS, 4, shard, BLOCK), BF),
+        ("g_c", (WHOLE_UNITS, 3, shard, BLOCK), BF),
+        ("h_out", (HALF_UNITS, 16, shard, HALF), BF), ("h", (HALF_UNITS, 16, shard, HALF), BF),
+        ("h_a", (HALF_UNITS, 8, shard, HALF), BF), ("h_b", (HALF_UNITS, 4, shard, HALF), BF),
+        ("h_c", (HALF_UNITS, 3, shard, HALF), BF),
         ("v_out", (2, 16, BLOCK), F32), ("v_own", (2, 16, BLOCK), F32),
         ("v_in", (2, 2 + nz, 16, BLOCK), F32), ("v_sum", (2, 3, 16, BLOCK), F32),
     ]
     n_weights = 8 + chunks
     sems = [
-        ("in_sem", (16 + chunks,)), ("w_send", (n_weights,)), ("w_recv", (n_weights,)),
-        ("core_send", (UNITS,)), ("core_recv", (UNITS,)), ("a_send", (UNITS,)), ("a_recv", (UNITS,)),
-        ("b_send", (UNITS,)), ("b_recv", (UNITS,)), ("c_send", (UNITS, 3)), ("c_recv", (UNITS, 3)),
-        ("v_send", (2, 2 + nz)), ("v_recv", (2, 2 + nz)),
+        ("in_sem", (16 + chunks,)), ("w_send", (n_weights,)), ("w_recv", (n_weights,)), ("sent", (4, 2)),
+        ("core_recv", (UNITS,)), ("a_recv", (UNITS,)), ("b_recv", (UNITS,)), ("c_recv", (UNITS,)),
+        ("v_send", (2, 4)), ("v_recv", (2, 4)),
     ]
     operands = [
         ("counts", region_counts), ("x_h", inputs), ("cot_h", cotangent), ("wq_h", w_query), ("wk_h", w_key),

time: 63.3 us -> 57.8 us (0.913)
  Pallas kernels: 62.3 us -> 56.8 us
    pallas_call x1, Pallas kernels: 60.7 us -> 55.2 us  [layer_by_items(): pl.pallas_call(functools.partial(layer_kernel, (items, length, rows_pad,...]
where the time goes in v4:
time: 57.8 us; the launch traced here: 57.7 us
  Pallas kernels  56.8 us (98%)
  between operations  0.85 us (1%)
    pallas_call x1, Pallas kernels, layer_by_items(): pl.pallas_call(functools.partial(layer_kernel, (items, length, rows_pad,...  55.2 us
    pallas_call x1, Pallas kernels, layer_by_items(): pl.pallas_call(functools.partial(hand_over, count), out_shape=shapes, in_...  1.64 us

profile of v4, /device:TPU:0, one launch (start us, length us, event | category | flops | bytes accessed | tf_op | source)
XLA Modules:
  0.0 57.7 jit_solution(348728305134298093)
XLA Ops:
  0.7 55.2 %layer.1 = (bf16[684,512]{1,0:T(8,128)(2,1)S(1)}, f32[684,512]{1,0:T(8,128)S(1)}, f32[32,256]{1,0:T(8,128)S(1)}, f32[1,256]{1,0:T(1,128)S(1)}, f32[32,256]{1,0:T...) custom-call(s32[6]{0:T(128)} %refs_0_.1, ...), custom_call_target="tpu_custom_call" | custom-call | tf_op jit(solution)/shard_map/layer/pallas_call | solution.py:1009
  55.8 1.6 %hand_over.1 = (bf16[684,512]{1,0:T(8,128)(2,1)}, f32[684,512]{1,0:T(8,128)}, f32[32,256]{1,0:T(8,128)}, f32[1,256]{1,0:T(1,128)}, f32[32,256]{1,0:T(8,128)}, /*...) custom-call(bf16[684,512]{1,0:T(8,128)(2,1)S(1)} %get-tuple-element., ...), custom_call_target="tpu_custom_call" | custom-call | tf_op jit(solution)/shard_map/hand_over/pallas_call | solution.py:1020

commit v5 on v4

--- a/solution.py
+++ b/solution.py
@@ -252,7 +252,7 @@
 WHOLE_UNITS, HALF_UNITS = 9, 6
 UNITS = WHOLE_UNITS + HALF_UNITS
 X_FIRST, Y_FIRST, Z_FIRST = 0, 1, 2
-ORDER = (0, 1, 2, 0, 1, 2, 1, 1, 2, 0, 1, 0, 1, 0, 1)
+ORDER = (0, 1, 2, 0, 1, 2, 0, 1, 0, 1, 0, 1, 0, 1, 0)
 PLAN = {
     13: (('M', 0, 1, 2, 3),),
     14: (('A', 0, 1),),
@@ -262,16 +262,15 @@
     25: (('A', 5),),
     26: (('B', 0, 1), ('A', 6),),
     27: (('B', 2), ('A', 7),),
-    31: (('M', 8), ('D', -1), ('C', 1), ('B', 3, 4),),
-    41: (('D', 0), ('A', 8), ('C', 0), ('B', 5),),
+    31: (('M', 8), ('D', -1), ('B', 3, 4),),
+    41: (('D', 0), ('A', 8), ('C', 0, 1), ('B', 5),),
     43: (('M', 9, 10, 11, 12, 13, 14), ('E', -1), ('C', 2),),
     51: (('C', 4), ('B', 6),),
     53: (('D', 1), ('A', 9, 10, 11),),
-    61: (('B', 7),),
-    63: (('D', 2), ('E', 0), ('A', 12, 13, 14), ('C', 3), ('B', 8),),
-    71: (('C', 5, 6), ('B', 9, 10, 11),),
-    72: (('C', 7),),
-    73: (('E', 1), ('B', 12, 13, 14), ('F', 0, 1, 2), ('C', 9, 10, 11), ('D', 3), ('E', 2), ('F', 3, 4), ('C', 12, 13, 14), ('C', 8), ('F', 5, 6, 7), ('F', 8, 9, 10, 11, 12, 13, 14), ('E', 3), ('D', 4), ('E', 4),),
+    63: (('E', 0), ('B', 8, 7), ('A', 12, 13, 14), ('C', 3, 6, 5),),
+    71: (('D', 2), ('B', 9, 10),),
+    72: (('B', 11), ('C', 7, 8),),
+    73: (('E', 1), ('B', 12, 13, 14), ('F', 0, 1, 2), ('C', 9, 10, 11), ('E', 2), ('D', 3), ('F', 3, 4), ('C', 12, 13, 14), ('F', 5, 6, 7, 8), ('F', 9, 10, 11, 12, 13, 14), ('E', 3), ('D', 4), ('E', 4),),
     20: (('A', 2, 3),),
 }
 

time: 57.8 us -> 56.4 us (0.976)
  Pallas kernels: 56.8 us -> 55.4 us
    pallas_call x1, Pallas kernels: 55.2 us -> 53.7 us  [layer_by_items(): pl.pallas_call(functools.partial(layer_kernel, (items, length, rows_pad,...]
where the time goes in v5:
time: 56.4 us; the launch traced here: 56.2 us
  Pallas kernels  55.4 us (98%)
  between operations  0.85 us (2%)
    pallas_call x1, Pallas kernels, layer_by_items(): pl.pallas_call(functools.partial(layer_kernel, (items, length, rows_pad,...  53.7 us
    pallas_call x1, Pallas kernels, layer_by_items(): pl.pallas_call(functools.partial(hand_over, count), out_shape=shapes, in_...  1.64 us

profile of v5, /device:TPU:0, one launch (start us, length us, event | category | flops | bytes accessed | tf_op | source)
XLA Modules:
  0.0 56.2 jit_solution(17483193149842534054)
XLA Ops:
  0.7 53.7 %layer.1 = (bf16[684,512]{1,0:T(8,128)(2,1)S(1)}, f32[684,512]{1,0:T(8,128)S(1)}, f32[32,256]{1,0:T(8,128)S(1)}, f32[1,256]{1,0:T(1,128)S(1)}, f32[32,256]{1,0:T...) custom-call(s32[6]{0:T(128)} %refs_0_.1, ...), custom_call_target="tpu_custom_call" | custom-call | tf_op jit(solution)/shard_map/layer/pallas_call | solution.py:1008
  54.4 1.6 %hand_over.1 = (bf16[684,512]{1,0:T(8,128)(2,1)}, f32[684,512]{1,0:T(8,128)}, f32[32,256]{1,0:T(8,128)}, f32[1,256]{1,0:T(1,128)}, f32[32,256]{1,0:T(8,128)}, /*...) custom-call(bf16[684,512]{1,0:T(8,128)(2,1)S(1)} %get-tuple-element., ...), custom_call_target="tpu_custom_call" | custom-call | tf_op jit(solution)/shard_map/hand_over/pallas_call | solution.py:1019

commit v6 on v5

--- a/solution.py
+++ b/solution.py
@@ -265,8 +265,8 @@
     31: (('M', 8), ('D', -1), ('B', 3, 4),),
     41: (('D', 0), ('A', 8), ('C', 0, 1), ('B', 5),),
     43: (('M', 9, 10, 11, 12, 13, 14), ('E', -1), ('C', 2),),
-    51: (('C', 4), ('B', 6),),
-    53: (('D', 1), ('A', 9, 10, 11),),
+    51: (('B', 6),),
+    53: (('D', 1), ('C', 4), ('A', 9, 10, 11),),
     63: (('E', 0), ('B', 8, 7), ('A', 12, 13, 14), ('C', 3, 6, 5),),
     71: (('D', 2), ('B', 9, 10),),
     72: (('B', 11), ('C', 7, 8),),
@@ -311,8 +311,16 @@
         local.append(copy)
         return copy
 
+    def bring_parts(parts, whole):
+        sem = r.in_sem.at[len(local)]
+        for src, dst in parts:
+            pltpu.make_async_copy(src, dst, sem).start()
+        copy = pltpu.make_async_copy(whole, whole, sem)
+        local.append(copy)
+        return copy
+
     c_x = bring(r.x_h, r.x_raw)
-    c_w = [bring(src, r.wqkv.at[0, k]) for k, src in enumerate((r.wq_h, r.wk_h, r.wv_h))]
+    c_w = [bring_parts([(src, r.wqkv.at[0, k]) for k, src in enumerate((r.wq_h, r.wk_h, r.wv_h))], r.wqkv.at[0])]
     c_p = [bring(r.b_query_h, r.bias_q.at[0]), bring(r.b_value_h, r.bias_v.at[0]), bring(r.b_up_h, r.bias_u.at[0])]
 
     barrier = pltpu.get_barrier_semaphore()
@@ -324,7 +332,8 @@
         (r.b_down_h, r.b_down), (r.gain_two_h, r.gain_two), (r.shift_two_h, r.shift_two))
     c_vec = [bring(src, dst) for src, dst in vectors]
     c_wo = bring(r.wo_h, r.wo.at[0])
-    c_wu = [bring(r.wu_h.at[:, pl.ds(c * BLOCK, BLOCK)], r.wu.at[c]) for c in range(chunks)]
+    up_blocks = [r.wu_h.at[:, pl.ds(c * BLOCK, BLOCK)] for c in range(chunks)]
+    c_wu = [bring_parts([(src, r.wu.at[c]) for c, src in enumerate(up_blocks)], r.wu.at[pl.ds(0, chunks)])]
     c_wd = bring(r.wd_h, r.wd.at[pl.ds(0, chunks)])
     full_rows = r.x_h.shape[0]
     base = items * length // 8 * 8
@@ -394,11 +403,25 @@
         remote.append(copy)
         return copy
 
-    s_w = [send_weight(src, r.wqkv.at[1, k]) for k, src in enumerate((r.wq_h, r.wk_h, r.wv_h))]
+    def send_parts(parts, whole):
+        k = len(remote)
+
+        def copy_of(src, dst):
+            return pltpu.make_async_remote_copy(
+                src_ref=src, dst_ref=dst, send_sem=r.w_send.at[k], recv_sem=r.w_recv.at[k],
+                device_id=core, device_id_type=MESH)
+
+        for src, dst in parts:
+            copy_of(src, dst).start()
+        copy = copy_of(whole, whole)
+        remote.append(copy)
+        return copy
+
+    s_w = [send_parts([(src, r.wqkv.at[1, k]) for k, src in enumerate((r.wq_h, r.wk_h, r.wv_h))], r.wqkv.at[1])]
     s_w += [send_weight(src, dst.at[1]) for src, dst in (
         (r.b_query_h, r.bias_q), (r.b_value_h, r.bias_v), (r.b_up_h, r.bias_u))]
     s_wo = send_weight(r.wo_h, r.wo.at[1])
-    s_wu = [send_weight(r.wu_h.at[:, pl.ds(c * BLOCK, BLOCK)], r.wu.at[chunks + c]) for c in range(chunks)]
+    s_wu = [send_parts([(src, r.wu.at[chunks + c]) for c, src in enumerate(up_blocks)], r.wu.at[pl.ds(chunks, chunks)])]
     s_wd = send_weight(r.wd_h, r.wd.at[pl.ds(chunks, chunks)])
 
     def project(slot, k):
@@ -490,9 +513,10 @@
         r.inv1[rows, :] = jnp.broadcast_to(inverse, (rows_pad, 128))
         r.hlow[rows, :] = (normed * r.gain_one[...] + r.shift_one[...]).astype(BF)
 
+    attended(0)
     for i in range(items):
-        attended(i)
-    for i in range(items):
+        if i + 1 < items:
+            attended(i + 1)
         first_norm(i)
 
     for c in c_wu + [c_wd]:
@@ -977,9 +1001,9 @@
         ("v_out", (2, 16, BLOCK), F32), ("v_own", (2, 16, BLOCK), F32),
         ("v_in", (2, 2 + nz, 16, BLOCK), F32), ("v_sum", (2, 3, 16, BLOCK), F32),
     ]
-    n_weights = 8 + chunks
+    n_weights = 7
     sems = [
-        ("in_sem", (16 + chunks,)), ("w_send", (n_weights,)), ("w_recv", (n_weights,)), ("sent", (4, 2)),
+        ("in_sem", (15,)), ("w_send", (n_weights,)), ("w_recv", (n_weights,)), ("sent", (4, 2)),
         ("core_recv", (UNITS,)), ("a_recv", (UNITS,)), ("b_recv", (UNITS,)), ("c_recv", (UNITS,)),
         ("v_send", (2, 4)), ("v_recv", (2, 4)),
     ]

time: 56.4 us -> 56.1 us (level)
  no operation moved by 1% of the time
where the time goes in v6:
time: 56.1 us; the launch traced here: 56 us
  Pallas kernels  55.1 us (98%)
  between operations  0.85 us (2%)
    pallas_call x1, Pallas kernels, layer_by_items(): pl.pallas_call(functools.partial(layer_kernel, (items, length, rows_pad,...  53.5 us
    pallas_call x1, Pallas kernels, layer_by_items(): pl.pallas_call(functools.partial(hand_over, count), out_shape=shapes, in_...  1.64 us

profile of v6, /device:TPU:0, one launch (start us, length us, event | category | flops | bytes accessed | tf_op | source)
XLA Modules:
  0.0 56.0 jit_solution(4609567283126559697)
XLA Ops:
  0.7 53.5 %layer.1 = (bf16[684,512]{1,0:T(8,128)(2,1)S(1)}, f32[684,512]{1,0:T(8,128)S(1)}, f32[32,256]{1,0:T(8,128)S(1)}, f32[1,256]{1,0:T(1,128)S(1)}, f32[32,256]{1,0:T...) custom-call(s32[6]{0:T(128)} %refs_0_.1, ...), custom_call_target="tpu_custom_call" | custom-call | tf_op jit(solution)/shard_map/layer/pallas_call | solution.py:1032
  54.1 1.6 %hand_over.1 = (bf16[684,512]{1,0:T(8,128)(2,1)}, f32[684,512]{1,0:T(8,128)}, f32[32,256]{1,0:T(8,128)}, f32[1,256]{1,0:T(1,128)}, f32[32,256]{1,0:T(8,128)}, /*...) custom-call(bf16[684,512]{1,0:T(8,128)(2,1)S(1)} %get-tuple-element., ...), custom_call_target="tpu_custom_call" | custom-call | tf_op jit(solution)/shard_map/hand_over/pallas_call | solution.py:1043
